TPU v7x, 512 devices: a whole 4x8x8 slice. The times are simulated.
512 devices in a mesh: depth: 64 (over y, z_hi, core), res: 8 (over z_lo, x).
Axes of the slice: x: 4, y: 8, z: 8 (z_hi: 4, z_lo: 2; z = z_hi * 2 + z_lo), core: 2. Of those that a mesh axis runs over, the one named last changes fastest.
Arguments:
- row_q: bfloat16 [128, 512, 768], P('depth', 'res'), may hold values from -22 to 22
- row_k: bfloat16 [128, 512, 768], P('depth', 'res'), may hold values from -5 to 5
- row_v: bfloat16 [128, 512, 768], P('depth', 'res'), may hold values from -5 to 5
- col_q: bfloat16 [128, 512, 768], P('depth', 'res'), may hold values from -200 to 200
- col_k: bfloat16 [128, 512, 768], P('depth', 'res'), may hold values from -5 to 5
- col_v: bfloat16 [128, 512, 768], P('depth', 'res'), may hold values from -5 to 5
- cotangent: bfloat16 [128, 512, 768], P('depth', 'res'), may hold values from -5 to 5
Outputs:
- update: bfloat16 [128, 512, 768], P('depth', 'res')
- grad_row_q: bfloat16 [128, 512, 768], P('depth', 'res')
- grad_row_k: bfloat16 [128, 512, 768], P('depth', 'res')
- grad_row_v: bfloat16 [128, 512, 768], P('depth', 'res')
- grad_col_q: bfloat16 [128, 512, 768], P('depth', 'res')
- grad_col_k: bfloat16 [128, 512, 768], P('depth', 'res')
- grad_col_v: bfloat16 [128, 512, 768], P('depth', 'res')
All inputs are finite; a program needn't handle non-finite values.
Results may differ from a plain program's by a relative error of at most 0.007.
Values may be sent and summed in bfloat16 or wider, within the bound.
No kernel may reach another device: no remote copies, remote signals or barrier semaphores. Data moves between devices by JAX's collectives and lax.ppermute only.
A program may use at most 64 MiB of HBM per device.

v0:
```python
import math

import jax
import jax.numpy as jnp
from jax import lax
from jax.sharding import PartitionSpec as P

H = 12
DH = 64


def split_heads(array):
    return array.reshape(array.shape[0], array.shape[1], H, DH)


def join_heads(array):
    return array.reshape(array.shape[0], array.shape[1], H * DH)


def to_heads(array):
    seqs, cols = (array.shape[0], array.shape[1])
    return array.reshape(seqs, cols, H, DH).transpose(2, 1, 0, 3).reshape(H, cols, seqs * DH)


def from_heads(array, seqs):
    cols = array.shape[1]
    return array.reshape(H, cols, seqs, DH).transpose(2, 1, 0, 3).reshape(seqs, cols, H * DH)


def on_device(row_q, row_k, row_v, col_q, col_k, col_v, cotangent):
    bf = jnp.bfloat16
    f32 = jnp.float32
    seqs_dev = row_q.shape[0]
    total_rows = seqs_dev * lax.axis_size("depth")
    row_scale = 1.0 / math.sqrt(DH) / math.sqrt(total_rows)
    col_scale = 1.0 / math.sqrt(DH)
    query_h = to_heads(row_q)
    grads_h = to_heads(cotangent)
    keys_all, values_all = (
        lax.all_gather(to_heads(row_k), "res", axis=1, tiled=True),
        lax.all_gather(to_heads(row_v), "res", axis=1, tiled=True),
    )
    logit_part = (
        jnp.einsum("hik,hjk->hij", query_h, keys_all, preferred_element_type=f32) * row_scale
    )
    logits = lax.psum(logit_part, "depth")
    probs = jax.nn.softmax(logits, axis=-1)
    probs_b = probs.astype(bf)
    dprob_part = jnp.einsum("hik,hjk->hij", grads_h, values_all, preferred_element_type=f32)
    dprobs = lax.psum(dprob_part, "depth")
    dlogits = (
        probs * (dprobs - jnp.sum(probs * dprobs, axis=-1, keepdims=True)) * row_scale
    ).astype(bf)
    row_out = jnp.einsum("hij,hjk->hik", probs_b, values_all, preferred_element_type=f32)
    grad_rq = jnp.einsum("hij,hjk->hik", dlogits, keys_all, preferred_element_type=f32).astype(bf)
    query_all, grads_all = (
        lax.all_gather(query_h, "res", axis=1, tiled=True),
        lax.all_gather(grads_h, "res", axis=1, tiled=True),
    )
    probs_cols, dlogit_cols = (
        lax.all_to_all(probs_b, "res", split_axis=2, concat_axis=1, tiled=True),
        lax.all_to_all(dlogits, "res", split_axis=2, concat_axis=1, tiled=True),
    )
    grad_rk = jnp.einsum("hij,hik->hjk", dlogit_cols, query_all, preferred_element_type=f32).astype(
        bf
    )
    grad_rv = jnp.einsum("hij,hik->hjk", probs_cols, grads_all, preferred_element_type=f32).astype(
        bf
    )
    c_query, c_keys, c_values, c_grads = (
        lax.all_to_all(col_q, "depth", split_axis=1, concat_axis=0, tiled=True),
        lax.all_to_all(col_k, "depth", split_axis=1, concat_axis=0, tiled=True),
        lax.all_to_all(col_v, "depth", split_axis=1, concat_axis=0, tiled=True),
        lax.all_to_all(cotangent, "depth", split_axis=1, concat_axis=0, tiled=True),
    )
    c_query = split_heads(c_query)
    c_keys = split_heads(c_keys)
    c_values = split_heads(c_values)
    c_grads = split_heads(c_grads)
    c_logits = (
        jnp.einsum("rchd,schd->chrs", c_query, c_keys, preferred_element_type=f32) * col_scale
    )
    c_probs = jax.nn.softmax(c_logits, axis=-1)
    c_probs_b = c_probs.astype(bf)
    c_out = jnp.einsum("chrs,schd->rchd", c_probs_b, c_values, preferred_element_type=f32).astype(
        bf
    )
    c_dprobs = jnp.einsum("rchd,schd->chrs", c_grads, c_values, preferred_element_type=f32)
    c_dlogits = (
        c_probs * (c_dprobs - jnp.sum(c_probs * c_dprobs, axis=-1, keepdims=True)) * col_scale
    ).astype(bf)
    c_gq = jnp.einsum("chrs,schd->rchd", c_dlogits, c_keys, preferred_element_type=f32).astype(bf)
    c_gk = jnp.einsum("chrs,rchd->schd", c_dlogits, c_query, preferred_element_type=f32).astype(bf)
    c_gv = jnp.einsum("chrs,rchd->schd", c_probs_b, c_grads, preferred_element_type=f32).astype(bf)
    col_out, grad_cq, grad_ck, grad_cv = (
        lax.all_to_all(join_heads(c_out), "depth", split_axis=0, concat_axis=1, tiled=True),
        lax.all_to_all(join_heads(c_gq), "depth", split_axis=0, concat_axis=1, tiled=True),
        lax.all_to_all(join_heads(c_gk), "depth", split_axis=0, concat_axis=1, tiled=True),
        lax.all_to_all(join_heads(c_gv), "depth", split_axis=0, concat_axis=1, tiled=True),
    )
    update = (from_heads(row_out, seqs_dev) + col_out.astype(f32)).astype(bf)
    return (
        update,
        from_heads(grad_rq, seqs_dev),
        from_heads(grad_rk, seqs_dev),
        from_heads(grad_rv, seqs_dev),
        grad_cq,
        grad_ck,
        grad_cv,
    )


def solution(mesh):
    in_specs = (
        P("depth", "res", None),
        P("depth", "res", None),
        P("depth", "res", None),
        P("depth", "res", None),
        P("depth", "res", None),
        P("depth", "res", None),
        P("depth", "res", None),
    )
    out_specs = (
        P("depth", "res", None),
        P("depth", "res", None),
        P("depth", "res", None),
        P("depth", "res", None),
        P("depth", "res", None),
        P("depth", "res", None),
        P("depth", "res", None),
    )
    return jax.shard_map(
        on_device, mesh=mesh, in_specs=in_specs, out_specs=out_specs, check_vma=False
    )
```

profile of v0, /device:TPU:1, one launch (start us, length us, event | category | flops | bytes accessed | tf_op | source)
XLA Modules:
  0.0 796.0 jit_solution(15077642125756702746)
XLA Ops:
  13.6 42.5 %all-gather.5.cloned.1.call-done = bf16[12,512,128]{2,1,0:T(8,128)(2,1)} async-done(((bf16[12,64,128]{2,1,0:T(8,128)(2,1)}), bf16[12,512,128]{2,1,0:T(8,128)(2,1)}) %all-gather.5.cloned.1.call-update) | async-done | bytes 1572880 | tf_op jit(solution)/shard_map/all_gather | solution.py:40
  56.1 3.3 convolution_multiply_fusion
  59.4 44.6 %all-gather.7.cloned.1.call-done = bf16[12,512,128]{2,1,0:T(8,128)(2,1)} async-done(((bf16[12,64,128]{2,1,0:T(8,128)(2,1)}), bf16[12,512,128]{2,1,0:T(8,128)(2,1)}) %all-gather.7.cloned.1.call-update) | async-done | bytes 1572880 | tf_op jit(solution)/shard_map/all_gather | solution.py:41
  103.9 3.2 fusion.38
  109.0 18.7 %all-to-all-start.2 = ((bf16[2,64,768]{2,0,1:T(2,128)(2,1)}), bf16[2,64,768]{2,0,1:T(2,128)(2,1)S(1)}, u32[]{:S(2)}, u32[]{:S(2)}) async-start(bf16[2,64,768]{2,0,1:T(2,128)(2,1)} %copy.74), calls=%async_computation.2 | async-start | bytes 393216 | tf_op jit(solution)/shard_map/all_to_all | solution.py:73
  128.6 13.5 %all-to-all-done.2 = bf16[2,64,768]{2,0,1:T(2,128)(2,1)S(1)} async-done(((bf16[2,64,768]{2,0,1:T(2,128)(2,1)}), bf16[2,64,768]{2,0,1:T(2,128)(2,1)S(1)}, u32[]{:S(2)}, u32[]{:S(2)}) %all-to-all-start.2) | async-done | bytes 196640 | tf_op jit(solution)/shard_map/all_to_all | solution.py:73
  142.2 4.5 all-to-all-start
  147.6 13.6 %all-to-all-done = bf16[2,64,768]{2,0,1:T(2,128)(2,1)S(1)} async-done(((bf16[2,64,768]{2,0,1:T(2,128)(2,1)}), bf16[2,64,768]{2,0,1:T(2,128)(2,1)S(1)}, u32[]{:S(2)}, u32[]{:S(2)}) %all-to-all-start) | async-done | bytes 196640 | tf_op jit(solution)/shard_map/all_to_all | solution.py:71
  161.2 4.4 all-to-all-start.1
  168.4 11.8 %all-to-all-done.1 = bf16[2,64,768]{2,0,1:T(2,128)(2,1)S(1)} async-done(((bf16[2,64,768]{2,0,1:T(2,128)(2,1)}), bf16[2,64,768]{2,0,1:T(2,128)(2,1)S(1)}, u32[]{:S(2)}, u32[]{:S(2)}) %all-to-all-start.1) | async-done | bytes 196640 | tf_op jit(solution)/shard_map/all_to_all | solution.py:72
  180.2 4.7 all-to-all-start.6
  188.8 10.5 %all-to-all-done.6 = bf16[2,64,768]{2,0,1:T(2,128)(2,1)S(1)} async-done(((bf16[2,64,768]{2,0,1:T(2,128)(2,1)}), bf16[2,64,768]{2,0,1:T(2,128)(2,1)S(1)}, u32[]{:S(2)}, u32[]{:S(2)}) %all-to-all-start.6) | async-done | bytes 196640 | tf_op jit(solution)/shard_map/all_to_all | solution.py:74
  199.4 4.5 all-to-all-start.3
  206.9 11.6 %all-to-all-done.3 = bf16[64,2,768]{2,1,0:T(2,128)(2,1)S(1)} async-done(((bf16[64,2,768]{2,1,0:T(2,128)(2,1)}), bf16[64,2,768]{2,1,0:T(2,128)(2,1)S(1)}, u32[]{:S(2)}, u32[]{:S(2)}) %all-to-all-start.3) | async-done | bytes 196640 | tf_op jit(solution)/shard_map/all_to_all | solution.py:96
  218.4 4.4 all-to-all-start.7
  224.9 12.6 %all-to-all-done.7 = bf16[64,2,768]{2,1,0:T(2,128)(2,1)S(1)} async-done(((bf16[64,2,768]{2,1,0:T(2,128)(2,1)}), bf16[64,2,768]{2,1,0:T(2,128)(2,1)S(1)}, u32[]{:S(2)}, u32[]{:S(2)}) %all-to-all-start.7) | async-done | bytes 196640 | tf_op jit(solution)/shard_map/all_to_all | solution.py:97
  237.5 4.4 all-to-all-start.8
  244.3 441.9 %all-reduce.3.cloned.1.call-done = (f32[12,64,512]{2,1,0:T(8,128)}, f32[12,64,512]{2,1,0:T(8,128)}) async-done(((f32[12,64,512]{2,1,0:T(8,128)}, f32[12,64,512]{2,1,0:T(8,128)}), (f32[12,64,512]{2,1,0:T(8,128)}, f32[12,64,512]{2,1,0:T(8,128)})) %all-reduce.3.cloned.1.call-update) | async-done | bytes 3145744 | tf_op jit(solution)/shard_map/psum | solution.py:46
  686.2 2.3 fusion.35
  688.6 8.7 %all-to-all-start.9 = ((bf16[64,2,768]{2,1,0:T(2,128)(2,1)}), bf16[64,2,768]{2,1,0:T(2,128)(2,1)S(1)}, u32[]{:S(2)}, u32[]{:S(2)}) async-start(bf16[64,2,768]{2,1,0:T(2,128)(2,1)} %reshape.195), calls=%async_computation.9 | async-start | bytes 393216 | tf_op jit(solution)/shard_map/all_to_all | solution.py:99
  697.2 7.1 multiply_convert_fusion
  704.4 2.9 copy.81
  709.3 2.4 all-to-all-done.9
  711.7 4.2 all-to-all-start.4
  720.7 12.0 %all-to-all-done.4 = bf16[8,2,24576]{2,1,0:T(2,128)(2,1)} async-done(((bf16[8,2,24576]{2,1,0:T(2,128)(2,1)}), bf16[8,2,24576]{2,1,0:T(2,128)(2,1)}, u32[]{:S(2)}, u32[]{:S(2)}) %all-to-all-start.4) | async-done | bytes 786464 | tf_op jit(solution)/shard_map/all_to_all | solution.py:62
  732.7 4.3 all-to-all-start.5
  740.5 2.9 reduce.7
  748.9 2.8 reduce.8
  758.4 7.5 convolution_convert_fusion.6
  768.0 3.2 reshape.188
  773.4 2.9 all_to_all.129
  783.0 2.7 all_to_all.133
  (124 shorter events, 60.5 us)
Async XLA Ops:
  7.2 2.7 copy-start.14
  7.2 48.9 %all-gather.5.cloned.1.call-start = ((), (), s32[]{:S(2)}) async-start(), calls=%async_computation.10 | async-start | bytes 1769472 | tf_op jit(solution)/shard_map/all_gather | solution.py:40
  8.9 2.7 copy-start.15
  9.9 94.1 %all-gather.7.cloned.1.call-start = ((), (), s32[]{:S(2)}) async-start(), calls=%async_computation.11 | async-start | bytes 1769472 | tf_op jit(solution)/shard_map/all_gather | solution.py:41
  10.7 1.9 copy-start.5
  11.6 674.6 %all-reduce.3.cloned.1.call-start = ((), (), s32[]{:S(2)}) async-start(), calls=%async_computation.14 | async-start | bytes 6291456 | tf_op jit(solution)/shard_map/psum | solution.py:46
  12.6 46.8 %copy-start.4 = (bf16[12,64,128]{2,1,0:T(8,128)(2,1)}, bf16[12,64,128]{2,1,0:T(8,128)(2,1)S(1)}, u32[]{:S(2)}) copy-start(bf16[12,64,128]{2,1,0:T(8,128)(2,1)S(1)} %reshape.157) | copy-start | bytes 589828
  13.6 90.4 %copy-start.3 = (bf16[12,64,128]{2,1,0:T(8,128)(2,1)}, bf16[12,64,128]{2,1,0:T(8,128)(2,1)S(1)}, u32[]{:S(2)}) copy-start(bf16[12,64,128]{2,1,0:T(8,128)(2,1)S(1)} %reshape.169) | copy-start | bytes 589828
  107.2 0.9 copy-start.11
  107.2 20.6 %copy-start.12 = (bf16[2,64,768]{2,1,0:T(8,128)(2,1)S(1)}, bf16[2,64,768]{2,1,0:T(8,128)(2,1)}, u32[]{:S(2)}) copy-start(bf16[2,64,768]{2,1,0:T(8,128)(2,1)} %param.10) | copy-start | bytes 589828
  108.1 38.6 %copy-start.13 = (bf16[2,64,768]{2,1,0:T(8,128)(2,1)S(1)}, bf16[2,64,768]{2,1,0:T(8,128)(2,1)}, u32[]{:S(2)}) copy-start(bf16[2,64,768]{2,1,0:T(8,128)(2,1)} %param.11) | copy-start | bytes 589828
  109.0 33.2 %all-to-all-start.2 = ((bf16[2,64,768]{2,0,1:T(2,128)(2,1)}), bf16[2,64,768]{2,0,1:T(2,128)(2,1)S(1)}, u32[]{:S(2)}, u32[]{:S(2)}) async-start(bf16[2,64,768]{2,0,1:T(2,128)(2,1)} %copy.74), calls=%async_computation.2 | async-start | bytes 393216 | tf_op jit(solution)/shard_map/all_to_all | solution.py:73
  142.2 19.0 %all-to-all-start = ((bf16[2,64,768]{2,0,1:T(2,128)(2,1)}), bf16[2,64,768]{2,0,1:T(2,128)(2,1)S(1)}, u32[]{:S(2)}, u32[]{:S(2)}) async-start(bf16[2,64,768]{2,0,1:T(2,128)(2,1)} %copy.70), calls=%async_computation | async-start | bytes 393216 | tf_op jit(solution)/shard_map/all_to_all | solution.py:71
  161.2 19.0 %all-to-all-start.1 = ((bf16[2,64,768]{2,0,1:T(2,128)(2,1)}), bf16[2,64,768]{2,0,1:T(2,128)(2,1)S(1)}, u32[]{:S(2)}, u32[]{:S(2)}) async-start(bf16[2,64,768]{2,0,1:T(2,128)(2,1)} %copy.71), calls=%async_computation.1 | async-start | bytes 393216 | tf_op jit(solution)/shard_map/all_to_all | solution.py:72
  165.6 610.8 %all-gather.9.cloned.1.call-start = ((), (), s32[]{:S(2)}) async-start(), calls=%async_computation.12 | async-start | bytes 1769472 | tf_op jit(solution)/shard_map/all_gather | solution.py:57
  180.2 19.2 %all-to-all-start.6 = ((bf16[2,64,768]{2,0,1:T(2,128)(2,1)}), bf16[2,64,768]{2,0,1:T(2,128)(2,1)S(1)}, u32[]{:S(2)}, u32[]{:S(2)}) async-start(bf16[2,64,768]{2,0,1:T(2,128)(2,1)} %copy.87), calls=%async_computation.6 | async-start | bytes 393216 | tf_op jit(solution)/shard_map/all_to_all | solution.py:74
  199.4 19.1 %all-to-all-start.3 = ((bf16[64,2,768]{2,1,0:T(2,128)(2,1)}), bf16[64,2,768]{2,1,0:T(2,128)(2,1)S(1)}, u32[]{:S(2)}, u32[]{:S(2)}) async-start(bf16[64,2,768]{2,1,0:T(2,128)(2,1)} %reshape.185), calls=%async_computation.3 | async-start | bytes 393216 | tf_op jit(solution)/shard_map/all_to_all | solution.py:96
  218.4 19.1 %all-to-all-start.7 = ((bf16[64,2,768]{2,1,0:T(2,128)(2,1)}), bf16[64,2,768]{2,1,0:T(2,128)(2,1)S(1)}, u32[]{:S(2)}, u32[]{:S(2)}) async-start(bf16[64,2,768]{2,1,0:T(2,128)(2,1)} %reshape.191), calls=%async_computation.7 | async-start | bytes 393216 | tf_op jit(solution)/shard_map/all_to_all | solution.py:97
  237.5 5.1 copy-start.6
  237.5 451.0 %all-to-all-start.8 = ((bf16[64,2,768]{2,1,0:T(2,128)(2,1)}), bf16[64,2,768]{2,1,0:T(2,128)(2,1)S(1)}, u32[]{:S(2)}, u32[]{:S(2)}) async-start(bf16[64,2,768]{2,1,0:T(2,128)(2,1)} %reshape.193), calls=%async_computation.8 | async-start | bytes 393216 | tf_op jit(solution)/shard_map/all_to_all | solution.py:98
  688.5 8.7 %copy-start = (f32[12,64,512]{2,1,0:T(8,128)}, f32[12,64,512]{2,1,0:T(8,128)S(1)}, u32[]{:S(2)}) copy-start(f32[12,64,512]{2,1,0:T(8,128)S(1)} %get-tuple-element.24) | copy-start | bytes 4718596
  688.5 8.7 %copy-start.8 = (bf16[64,2,768]{2,1,0:T(2,128)(2,1)}, bf16[64,2,768]{2,1,0:T(2,128)(2,1)S(1)}, u32[]{:S(2)}) copy-start(bf16[64,2,768]{2,1,0:T(2,128)(2,1)S(1)} %all-to-all-done.8) | copy-start | bytes 589828
  688.6 23.1 %all-to-all-start.9 = ((bf16[64,2,768]{2,1,0:T(2,128)(2,1)}), bf16[64,2,768]{2,1,0:T(2,128)(2,1)S(1)}, u32[]{:S(2)}, u32[]{:S(2)}) async-start(bf16[64,2,768]{2,1,0:T(2,128)(2,1)} %reshape.195), calls=%async_computation.9 | async-start | bytes 393216 | tf_op jit(solution)/shard_map/all_to_all | solution.py:99
  709.3 7.2 copy-start.1
  711.6 4.8 copy-start.10
  711.7 21.0 %all-to-all-start.4 = ((bf16[8,2,24576]{2,1,0:T(2,128)(2,1)}), bf16[8,2,24576]{2,1,0:T(2,128)(2,1)}, u32[]{:S(2)}, u32[]{:S(2)}) async-start(bf16[8,2,24576]{2,1,0:T(2,128)(2,1)} %reshape.187), calls=%async_computation.4 | async-start | bytes 1572864 | tf_op jit(solution)/shard_map/all_to_all | solution.py:62
  715.9 69.9 %all-gather.11.cloned.1.call-start = ((), (), s32[]{:S(2)}) async-start(), calls=%async_computation.13 | async-start | bytes 1769472 | tf_op jit(solution)/shard_map/all_gather | solution.py:58
  720.7 16.8 %copy-start.7 = (bf16[64,2,768]{2,1,0:T(2,128)(2,1)S(1)}, bf16[64,2,768]{2,1,0:T(2,128)(2,1)}, u32[]{:S(2)}) copy-start(bf16[64,2,768]{2,1,0:T(2,128)(2,1)} %copy-done.6) | copy-start | bytes 589828
  732.7 47.0 %all-to-all-start.5 = ((bf16[8,2,24576]{2,1,0:T(2,128)(2,1)}), bf16[8,2,24576]{2,1,0:T(2,128)(2,1)S(1)}, u32[]{:S(2)}, u32[]{:S(2)}) async-start(bf16[8,2,24576]{2,1,0:T(2,128)(2,1)} %reshape.189), calls=%async_computation.5 | async-start | bytes 1572864 | tf_op jit(solution)/shard_map/all_to_all | solution.py:61
  736.9 2.7 copy-start.9
  740.5 14.4 %copy-start.2 = (bf16[12,512,128]{2,1,0:T(8,128)(2,1)S(1)}, bf16[12,512,128]{2,1,0:T(8,128)(2,1)}, u32[]{:S(2)}) copy-start(bf16[12,512,128]{2,1,0:T(8,128)(2,1)} %all-gather.7.cloned.1.call-done) | copy-start | bytes 4718596
Sparse Core Ops, SparseCore 0:
  10.7 45.3 all-gather.4
  58.7 45.1 all-gather.6
  107.3 578.8 all-reduce.2
  688.9 45.1 all-gather.8
  736.3 42.6 all-gather.10
where the time goes:
time: 804 us; the launch traced here: 796 us
  waiting for transfers between devices  618 us (77%)
  starting transfers between devices  63.3 us (8%)
  local copies, waits for them, and re-layouts  57.9 us (7%)
  matrix products  21.6 us (3%)
  other arithmetic  20.5 us (3%)
  between operations  14.8 us (2%)
    psum x1, waiting for transfers between devices, on_device(): logits = lax.psum(logit_part, 'depth')  442 us
    all_gather x1, waiting for transfers between devices, on_device(): lax.all_gather(to_heads(row_v), 'res', axis=1, tiled=True)  44.6 us
    all_gather x1, waiting for transfers between devices, on_device(): lax.all_gather(to_heads(row_k), 'res', axis=1, tiled=True)  42.5 us
    unnamed x55, local copies, waits for them, and re-layouts  23.8 us
    all_to_all x1, starting transfers between devices, on_device(): lax.all_to_all(col_v, 'depth', split_axis=1, concat_axis=0, tiled=True)  18.7 us
  transfers between devices with their start and end apart: 15, of which 11 were waited for; matrix products, arithmetic and copies ran while one was open for 10% of the time, Pallas kernels for 0%

commit v1 on v0

v1 whole, which is shorter than its diff:
```python
import math

import jax
import jax.numpy as jnp
from jax import lax
from jax.experimental import pallas as pl
from jax.experimental.pallas import tpu as pltpu
from jax.sharding import Mesh, PartitionSpec as P

H = 12
DH = 64
ROWS = 128
COLS = 512
HG = ("ylo", "core")
RED = ("yhi", "zhi")
DEP = ("yhi", "ylo", "zhi", "core")
RES = ("zlo", "x")
NHG = 4
HL = 3
NRED = 16
NRES = 8
CB = 64
QR = HL * CB // NRED
ROW_SCALE = 1.0 / math.sqrt(DH) / math.sqrt(ROWS)
COL_SCALE = 1.0 / math.sqrt(DH)
bf = jnp.bfloat16
f32 = jnp.float32


def call(body, out_shape, *args, flops=10**8):
    many = isinstance(out_shape, (list, tuple))
    outs = out_shape if many else [out_shape]
    nbytes = sum(math.prod(a.shape) * a.dtype.itemsize for a in list(args) + list(outs))
    return pl.pallas_call(
        body,
        out_shape=out_shape,
        in_specs=[pl.BlockSpec(memory_space=pltpu.VMEM)] * len(args),
        out_specs=[pl.BlockSpec(memory_space=pltpu.VMEM)] * len(outs)
        if many
        else pl.BlockSpec(memory_space=pltpu.VMEM),
        compiler_params=pltpu.CompilerParams(vmem_limit_bytes=40 * 2**20),
        cost_estimate=pl.CostEstimate(flops=flops, bytes_accessed=nbytes, transcendentals=0),
    )(*args)


def sds(shape, dtype):
    return jax.ShapeDtypeStruct(shape, dtype)


def dot(a, b, ca, cb):
    return lax.dot_general(a, b, (((ca,), (cb,)), ((), ())), preferred_element_type=f32)


def to_heads_kernel(*refs):
    out = refs[-1]
    for n, ref in enumerate(refs[:-1]):
        for h in range(H):
            a = ref[0, :, h * DH : (h + 1) * DH]
            b = ref[1, :, h * DH : (h + 1) * DH]
            out[h // HL, n, h % HL] = jnp.concatenate([a, b], axis=1)


def logits_kernel(mine, keys_values, out):
    for h in range(HL):
        parts = []
        for n, which in ((2, 0), (3, 1)):
            lhs = jnp.concatenate([mine[s, n, h] for s in range(NHG)], axis=1)
            rhs = jnp.concatenate(
                [
                    jnp.concatenate([keys_values[r, s, which, h] for r in range(NRES)], axis=0)
                    for s in range(NHG)
                ],
                axis=1,
            )
            parts.append(dot(lhs, rhs, 1, 1))
        for i in range(0, CB, 4):
            row = h * CB + i
            m, q = row // QR, row % QR
            out[m, q : q + 4, :] = parts[0][i : i + 4]
            out[m, QR + q : QR + q + 4, :] = parts[1][i : i + 4]


def softmax_kernel(parts, out):
    total = parts[0]
    for m in range(1, NRED):
        total = total + parts[m]
    logits = total[:QR] * ROW_SCALE
    dprobs = total[QR:]
    e = jnp.exp(logits - jnp.max(logits, axis=-1, keepdims=True))
    probs = e / jnp.sum(e, axis=-1, keepdims=True)
    dl = probs * (dprobs - jnp.sum(probs * dprobs, axis=-1, keepdims=True)) * ROW_SCALE
    both = jnp.concatenate([probs, dl], axis=0).astype(bf)
    for m in range(NRED):
        out[m] = both


def assemble_kernel(rows, probs, dlogits, by_key):
    parts = [rows[m].astype(f32) for m in range(NRED)]
    p = jnp.concatenate([a[:QR] for a in parts], axis=0).astype(bf)
    d = jnp.concatenate([a[QR:] for a in parts], axis=0).astype(bf)
    probs[...] = p
    dlogits[...] = d
    for r in range(NRES):
        by_key[r] = jnp.concatenate(
            [p[:, r * CB : (r + 1) * CB], d[:, r * CB : (r + 1) * CB]], axis=1
        )


def query_side_kernel(probs, dlogits, keys_values, out):
    for h in range(HL):
        for n, (lhs, which) in enumerate(((probs, 1), (dlogits, 0))):
            rhs = jnp.concatenate(
                [
                    jnp.concatenate([keys_values[r, s, which, h] for s in range(NHG)], axis=1)
                    for r in range(NRES)
                ],
                axis=0,
            )
            res = dot(lhs[h * CB : (h + 1) * CB, :], rhs, 1, 0).astype(bf)
            for s in range(NHG):
                out[s, n, h] = res[:, s * 2 * DH : (s + 1) * 2 * DH]


def key_side_kernel(by_query, queries, grads, out):
    for h in range(HL):
        lhs = jnp.concatenate(
            [by_query[r, h * CB : (h + 1) * CB, :] for r in range(NRES)], axis=0
        )
        for n, (ref, low) in enumerate(((queries, CB), (grads, 0))):
            rhs = jnp.concatenate(
                [
                    jnp.concatenate([ref[r, s, h] for s in range(NHG)], axis=1)
                    for r in range(NRES)
                ],
                axis=0,
            )
            res = dot(lhs, rhs, 0, 0)[low : low + CB].astype(bf)
            for s in range(NHG):
                out[s, n, h] = res[:, s * 2 * DH : (s + 1) * 2 * DH]


def column_kernel(query, keys, values, grads, out):
    lane = lax.broadcasted_iota(jnp.int32, (ROWS, 2 * DH), 1)
    first = lane < DH
    zero = jnp.zeros((ROWS, 2 * DH), bf)
    for pair in range(H // 2):
        at = slice(pair * 2 * DH, (pair + 1) * 2 * DH)
        q, k, v, g = (ref[:, at] for ref in (query, keys, values, grads))
        res = []
        for half in range(2):
            keep = first if half == 0 else jnp.logical_not(first)
            logits = dot(jnp.where(keep, q, zero), k, 1, 1) * COL_SCALE
            dprobs = dot(jnp.where(keep, g, zero), v, 1, 1)
            e = jnp.exp(logits - jnp.max(logits, axis=-1, keepdims=True))
            probs = e / jnp.sum(e, axis=-1, keepdims=True)
            dl = probs * (dprobs - jnp.sum(probs * dprobs, axis=-1, keepdims=True)) * COL_SCALE
            pb = probs.astype(bf)
            db = dl.astype(bf)
            res.append((dot(pb, v, 1, 0), dot(db, k, 1, 0), dot(db, q, 0, 0), dot(pb, g, 0, 0)))
        for n in range(4):
            out[n, :, at] = jnp.where(first, res[0][n], res[1][n]).astype(bf)


def finish_kernel(rows, col_out, update, grad_q, grad_k, grad_v):
    for pair in range(H // 2):
        for n, ref in enumerate((update, grad_q, grad_k, grad_v)):
            a, b = (rows[h // HL, n, h % HL] for h in (2 * pair, 2 * pair + 1))
            for r in range(2):
                got = jnp.concatenate(
                    [a[:, r * DH : (r + 1) * DH], b[:, r * DH : (r + 1) * DH]], axis=1
                )
                at = slice(pair * 2 * DH, (pair + 1) * 2 * DH)
                if n == 0:
                    got = (got.astype(f32) + col_out[r, :, at].astype(f32)).astype(bf)
                ref[r, :, at] = got


def swap(array, axes):
    return lax.all_to_all(array, axes, 0, 0, tiled=True)


def on_device(row_q, row_k, row_v, col_q, col_k, col_v, cotangent):
    dev = sds((2, CB, H * DH), bf)
    by_head = call(
        to_heads_kernel, sds((NHG, 4, HL, CB, 2 * DH), bf), row_k, row_v, row_q, cotangent
    )
    mine = swap(by_head, HG)
    queries = lax.all_gather(mine[:, 2], RES, axis=0)
    grads = lax.all_gather(mine[:, 3], RES, axis=0)
    own_kv = mine[:, :2]
    keys_values = swap(jnp.broadcast_to(own_kv, (NRES,) + own_kv.shape), RES)

    cols = jnp.stack([col_q, col_k, col_v, cotangent]).transpose(2, 0, 1, 3)
    cols = swap(cols.reshape(CB, 8, H * DH), DEP)
    cols = cols.reshape(CB, 4, 2, H * DH).transpose(1, 0, 2, 3).reshape(4, ROWS, H * DH)

    parts = call(logits_kernel, sds((NRED, 2 * QR, COLS), f32), mine, keys_values)
    parts = swap(parts, RED)
    rows = call(softmax_kernel, sds((NRED, 2 * QR, COLS), bf), parts)
    rows = swap(rows, RED)
    probs, dlogits, by_key = call(
        assemble_kernel,
        [
            sds((HL * CB, COLS), bf),
            sds((HL * CB, COLS), bf),
            sds((NRES, HL * CB, 2 * CB), bf),
        ],
        rows,
    )
    by_query = swap(by_key, RES)
    side = sds((NHG, 2, HL, CB, 2 * DH), bf)
    query_side = call(query_side_kernel, side, probs, dlogits, keys_values)

    done = call(column_kernel, sds((4, ROWS, H * DH), bf), cols[0], cols[1], cols[2], cols[3])
    done = done.reshape(4, CB, 2, H * DH).transpose(1, 0, 2, 3).reshape(CB, 8, H * DH)
    done = swap(done, DEP)
    done = done.reshape(CB, 4, 2, H * DH).transpose(1, 2, 0, 3)

    key_side = call(key_side_kernel, side, by_query, queries, grads)
    back = swap(jnp.concatenate([query_side, key_side], axis=1), HG)
    update, grad_rq, grad_rk, grad_rv = call(finish_kernel, [dev] * 4, back, done[0])
    return update, grad_rq, grad_rk, grad_rv, done[1], done[2], done[3]


def solution(mesh):
    fine = Mesh(
        mesh.devices.reshape(4, 2, 4, 2, 2, 4), ("yhi", "ylo", "zhi", "core", "zlo", "x")
    )
    spec = P(DEP, RES, None)
    return jax.shard_map(
        on_device, mesh=fine, in_specs=(spec,) * 7, out_specs=(spec,) * 7, check_vma=False
    )
```

time: 804 us -> 262 us (0.33)
  waiting for transfers between devices: 618 us -> 75.1 us
  blocking collectives: 0 us -> 59.3 us
  matrix products: 21.6 us -> 0 us
  other arithmetic: 20.5 us -> 2.3 us
  starting transfers between devices: 63.3 us -> 50.6 us
  Pallas kernels: 0 us -> 10.9 us
  local copies, waits for them, and re-layouts: 57.9 us -> 47.3 us
    psum x1 -> x0, waiting for transfers between devices: 442 us -> none  [on_device(): logits = lax.psum(logit_part, 'depth')]
    all_gather x4 -> x2, waiting for transfers between devices: 87.1 us -> 0.01 us  [the longest x1 0.01 us: on_device(): queries = lax.all_gather(mine[:, 2], RES, axis=0)]
    all_to_all x0 -> x2, blocking collectives: none -> 59.3 us  [swap(): return lax.all_to_all(array, axes, 0, 0, tiled=True)]
    dot_general x11 -> x0, matrix products: 21.1 us -> none  [the longest x1 7.5 us: on_device(): jnp.einsum('hij,hjk->hik', dlogits, keys_all, preferred_element_type=f32)]
    all_to_all x10 -> x6, waiting for transfers between devices: 88 us -> 74.3 us  [swap(): return lax.all_to_all(array, axes, 0, 0, tiled=True)]
    all_to_all x10 -> x6, starting transfers between devices: 62.9 us -> 50.5 us  [swap(): return lax.all_to_all(array, axes, 0, 0, tiled=True)]
    pallas_call x0 -> x8, Pallas kernels: none -> 10.9 us  [call(): pl.pallas_call(body, out_shape=out_shape, in_specs=[pl.BlockSpec(memory_s...]
    all_to_all x7 -> x2, local copies, waits for them, and re-layouts: 13.4 us -> 2.54 us  [swap(): return lax.all_to_all(array, axes, 0, 0, tiled=True)]
  transfers between devices with their start and end apart: 15 -> 8, of which waited for: 11 -> 5; matrix products, arithmetic and copies ran while one was open for 10% -> 12% of each run, Pallas kernels for 0% -> 3%
where the time goes in v1:
time: 262 us; the launch traced here: 260 us
  waiting for transfers between devices  75.1 us (29%)
  blocking collectives  59.3 us (23%)
  starting transfers between devices  50.6 us (19%)
  local copies, waits for them, and re-layouts  47.3 us (18%)
  between operations  14.2 us (5%)
  Pallas kernels  10.9 us (4%)
    all_to_all x6, waiting for transfers between devices, swap(): return lax.all_to_all(array, axes, 0, 0, tiled=True)  74.3 us
    all_to_all x2, blocking collectives, swap(): return lax.all_to_all(array, axes, 0, 0, tiled=True)  59.3 us
    all_to_all x6, starting transfers between devices, swap(): return lax.all_to_all(array, axes, 0, 0, tiled=True)  50.5 us
    unnamed x42, local copies, waits for them, and re-layouts  17.9 us
    pallas_call x8, Pallas kernels, call(): pl.pallas_call(body, out_shape=out_shape, in_specs=[pl.BlockSpec(memory_s...  10.9 us
    reshape x2, local copies, waits for them, and re-layouts, on_device(): done.reshape(4, CB, 2, H * DH).transpose(1, 0, 2, 3).reshape(CB, 8, H * DH)  5.81 us
  transfers between devices with their start and end apart: 8, of which 5 were waited for; matrix products, arithmetic and copies ran while one was open for 12% of the time, Pallas kernels for 3%

profile of v1, /device:TPU:1, one launch (start us, length us, event | category | flops | bytes accessed | tf_op | source)
XLA Modules:
  0.0 259.7 jit_solution(14879390688429064648)
XLA Ops:
  11.2 19.9 %all_to_all.40.mine = bf16[4,4,3,64,128]{4,3,2,1,0:T(8,128)(2,1)S(1)} all-to-all(bf16[4,4,3,64,128]{4,3,2,1,0:T(8,128)(2,1)S(1)} %shard_map.126), channel_id=1, replica_groups=mesh['yhi'=4,'ylo'=2,'zhi'=4,'core'=2,'zlo'=2,'x'=4] {'ylo','core'}, dimensions={0} | all-to-all | bytes 1572864 | tf_op jit(solution)/shard_map/all_to_all | solution.py:179
  31.9 39.4 %all_to_all.41.keys_values = bf16[8,4,2,3,64,128]{5,4,3,2,1,0:T(8,128)(2,1)S(1)} all-to-all(bf16[8,4,2,3,64,128]{5,4,3,2,1,0:T(8,128)(2,1)S(1)} %broadcast_in_dim.3), channel_id=1, replica_groups=mesh['yhi'=4,'ylo'=2,'zhi'=4,'core'=2,'zlo'=2,'x'=4] {'zlo','x'}, dimensions={0} | all-to-all | bytes 6291456 | tf_op jit(solution)/shard_map/all_to_all | solution.py:179
  73.3 11.6 %all-to-all-start.2 = ((f32[16,24,512]{2,1,0:T(8,128)}), f32[16,24,512]{2,1,0:T(8,128)}, u32[]{:S(2)}, u32[]{:S(2)}) async-start(f32[16,24,512]{2,1,0:T(8,128)} %copy-done.1), calls=%async_computation.2 | async-start | bytes 1572864 | tf_op jit(solution)/shard_map/all_to_all | solution.py:179
  84.9 1.8 fusion.1
  86.7 19.0 %all-to-all-done.2.parts = f32[16,24,512]{2,1,0:T(8,128)} async-done(((f32[16,24,512]{2,1,0:T(8,128)}), f32[16,24,512]{2,1,0:T(8,128)}, u32[]{:S(2)}, u32[]{:S(2)}) %all-to-all-start.2) | async-done | bytes 786464 | tf_op jit(solution)/shard_map/all_to_all | solution.py:179
  105.7 1.4 shard_map.128
  107.9 10.8 %all-to-all-start.3 = ((bf16[16,24,512]{2,1,0:T(8,128)(2,1)}), bf16[16,24,512]{2,1,0:T(8,128)(2,1)S(1)}, u32[]{:S(2)}, u32[]{:S(2)}) async-start(bf16[16,24,512]{2,1,0:T(8,128)(2,1)} %copy-done.3), calls=%async_computation.3 | async-start | bytes 786432 | tf_op jit(solution)/shard_map/all_to_all | solution.py:179
  118.7 1.3 pad_maximum_fusion.1
  120.0 1.3 copy.28
  121.3 10.0 %all-to-all-done.3.rows = bf16[16,24,512]{2,1,0:T(8,128)(2,1)S(1)} async-done(((bf16[16,24,512]{2,1,0:T(8,128)(2,1)}), bf16[16,24,512]{2,1,0:T(8,128)(2,1)S(1)}, u32[]{:S(2)}, u32[]{:S(2)}) %all-to-all-start.3) | async-done | bytes 393248 | tf_op jit(solution)/shard_map/all_to_all | solution.py:179
  131.3 13.0 %all-to-all-start.6 = ((bf16[64,8,768]{2,1,0:T(8,128)(2,1)}), bf16[64,8,768]{2,1,0:T(8,128)(2,1)}, u32[]{:S(2)}, u32[]{:S(2)}) async-start(bf16[64,8,768]{2,1,0:T(8,128)(2,1)} %copy.28), calls=%async_computation.6 | async-start | bytes 1572864 | tf_op jit(solution)/shard_map/all_to_all | solution.py:179
  147.4 20.8 %all-to-all-done.6 = bf16[64,8,768]{2,1,0:T(8,128)(2,1)} async-done(((bf16[64,8,768]{2,1,0:T(8,128)(2,1)}), bf16[64,8,768]{2,1,0:T(8,128)(2,1)}, u32[]{:S(2)}, u32[]{:S(2)}) %all-to-all-start.6) | async-done | bytes 786464 | tf_op jit(solution)/shard_map/all_to_all | solution.py:179
  168.2 3.5 %all-to-all-start.4 = ((bf16[8,192,128]{2,1,0:T(8,128)(2,1)}), bf16[8,192,128]{2,1,0:T(8,128)(2,1)S(1)}, u32[]{:S(2)}, u32[]{:S(2)}) async-start(bf16[8,192,128]{2,1,0:T(8,128)(2,1)} %copy-done.13), calls=%async_computation.4 | async-start | bytes 786432 | tf_op jit(solution)/shard_map/all_to_all | solution.py:179
  171.7 1.3 copy.21
  174.7 1.7 squeeze.24.query
  176.3 1.8 copy.23
  178.2 1.7 squeeze.25.keys
  179.8 1.8 copy.24
  181.6 1.7 squeeze.26.values
  183.3 1.8 copy.25
  185.1 1.7 squeeze.27.grads
  190.5 5.6 %shard_map.132 = bf16[4,128,768]{2,1,0:T(8,128)(2,1)S(1)} custom-call(bf16[128,768]{1,0:T(8,128)(2,1)S(1)} %copy-done.9, bf16[128,768]{1,0:T(8,128)(2,1)S(1)} %copy-done.10, bf16[128,768]{1,0:T(8,128)(2,1)S(1)} %copy-done.11, bf16[128,768]{1,0:T(8,128)(2,1)S(1)} %copy-done.12), custom_call_target="tpu_custom_call" | custom-call | flops 100000000 | bytes 1572864 | tf_op jit(solution)/shard_map/pallas_call | solution.py:34
  197.0 2.8 %reshape.40 = bf16[4,64,2,768]{3,2,1,0:T(2,128)(2,1)} reshape(bf16[4,128,768]{2,1,0:T(8,128)(2,1)} %copy-done.2) | data formatting | bytes 1572864 | tf_op jit(solution)/shard_map/reshape | solution.py:215
  199.8 2.6 copy.26
  202.4 3.0 %reshape.41 = bf16[64,8,768]{2,1,0:T(8,128)(2,1)} reshape(bf16[64,4,2,768]{3,2,1,0:T(2,128)(2,1)} %copy.26) | data formatting | bytes 1572864 | tf_op jit(solution)/shard_map/reshape | solution.py:215
  205.4 7.3 %all-to-all-start.7 = ((bf16[64,8,768]{2,1,0:T(8,128)(2,1)}), bf16[64,8,768]{2,1,0:T(8,128)(2,1)}, u32[]{:S(2)}, u32[]{:S(2)}) async-start(bf16[64,8,768]{2,1,0:T(8,128)(2,1)} %reshape.41), calls=%async_computation.7 | async-start | bytes 1572864 | tf_op jit(solution)/shard_map/all_to_all | solution.py:179
  215.9 1.4 copy-done.4
  217.3 1.4 copy-done.5
  220.7 15.8 %all-to-all-done.7 = bf16[64,8,768]{2,1,0:T(8,128)(2,1)} async-done(((bf16[64,8,768]{2,1,0:T(8,128)(2,1)}), bf16[64,8,768]{2,1,0:T(8,128)(2,1)}, u32[]{:S(2)}, u32[]{:S(2)}) %all-to-all-start.7) | async-done | bytes 786464 | tf_op jit(solution)/shard_map/all_to_all | solution.py:179
  236.5 4.5 %all-to-all-start.5 = ((bf16[4,4,3,64,128]{4,3,2,1,0:T(8,128)(2,1)}), bf16[4,4,3,64,128]{4,3,2,1,0:T(8,128)(2,1)S(1)}, u32[]{:S(2)}, u32[]{:S(2)}) async-start(bf16[4,4,3,64,128]{4,3,2,1,0:T(8,128)(2,1)} %pad_maximum_fusion), calls=%async_computation.5 | async-start | bytes 1572864 | tf_op jit(solution)/shard_map/all_to_all | solution.py:179
  241.0 1.3 copy.27
  243.1 8.7 %all-to-all-done.5.rows = bf16[4,4,3,64,128]{4,3,2,1,0:T(8,128)(2,1)S(1)} async-done(((bf16[4,4,3,64,128]{4,3,2,1,0:T(8,128)(2,1)}), bf16[4,4,3,64,128]{4,3,2,1,0:T(8,128)(2,1)S(1)}, u32[]{:S(2)}, u32[]{:S(2)}) %all-to-all-start.5) | async-done | bytes 786464 | tf_op jit(solution)/shard_map/all_to_all | solution.py:179
  (59 shorter events, 24.0 us)
Async XLA Ops:
  7.2 0.9 copy-start.8
  8.1 0.9 copy-start.14
  9.0 0.9 copy-start.15
  10.0 0.9 copy-start.16
  31.1 40.2 %copy-start = (bf16[4,4,3,64,128]{4,3,2,1,0:T(8,128)(2,1)}, bf16[4,4,3,64,128]{4,3,2,1,0:T(8,128)(2,1)S(1)}, u32[]{:S(2)}) copy-start(bf16[4,4,3,64,128]{4,3,2,1,0:T(8,128)(2,1)S(1)} %all_to_all.40.mine) | copy-start | bytes 2359300
  72.4 0.9 copy-start.1
  73.3 32.4 %all-to-all-start.2 = ((f32[16,24,512]{2,1,0:T(8,128)}), f32[16,24,512]{2,1,0:T(8,128)}, u32[]{:S(2)}, u32[]{:S(2)}) async-start(f32[16,24,512]{2,1,0:T(8,128)} %copy-done.1), calls=%async_computation.2 | async-start | bytes 1572864 | tf_op jit(solution)/shard_map/all_to_all | solution.py:179
  84.9 131.0 %all-gather.5.cloned.1.call-start = ((), (), s32[]{:S(2)}) async-start(), calls=%async_computation.8 | async-start | bytes 1769472 | tf_op jit(solution)/shard_map/all_gather | solution.py:188
  107.2 0.8 copy-start.3
  107.9 23.4 %all-to-all-start.3 = ((bf16[16,24,512]{2,1,0:T(8,128)(2,1)}), bf16[16,24,512]{2,1,0:T(8,128)(2,1)S(1)}, u32[]{:S(2)}, u32[]{:S(2)}) async-start(bf16[16,24,512]{2,1,0:T(8,128)(2,1)} %copy-done.3), calls=%async_computation.3 | async-start | bytes 786432 | tf_op jit(solution)/shard_map/all_to_all | solution.py:179
  131.3 36.9 %all-to-all-start.6 = ((bf16[64,8,768]{2,1,0:T(8,128)(2,1)}), bf16[64,8,768]{2,1,0:T(8,128)(2,1)}, u32[]{:S(2)}, u32[]{:S(2)}) async-start(bf16[64,8,768]{2,1,0:T(8,128)(2,1)} %copy.28), calls=%async_computation.6 | async-start | bytes 1572864 | tf_op jit(solution)/shard_map/all_to_all | solution.py:179
  144.4 71.5 %all-gather.7.cloned.1.call-start = ((), (), s32[]{:S(2)}) async-start(), calls=%async_computation.9 | async-start | bytes 1769472 | tf_op jit(solution)/shard_map/all_gather | solution.py:189
  145.3 0.8 copy-start.13
  146.1 0.7 copy-start.17
  146.8 0.7 copy-start.19
  168.2 37.1 %all-to-all-start.4 = ((bf16[8,192,128]{2,1,0:T(8,128)(2,1)}), bf16[8,192,128]{2,1,0:T(8,128)(2,1)S(1)}, u32[]{:S(2)}, u32[]{:S(2)}) async-start(bf16[8,192,128]{2,1,0:T(8,128)(2,1)} %copy-done.13), calls=%async_computation.4 | async-start | bytes 786432 | tf_op jit(solution)/shard_map/all_to_all | solution.py:179
  186.8 0.9 copy-start.9
  187.7 0.9 copy-start.10
  188.7 0.9 copy-start.11
  189.6 0.9 copy-start.12
  196.1 0.9 copy-start.2
  205.4 31.2 %all-to-all-start.7 = ((bf16[64,8,768]{2,1,0:T(8,128)(2,1)}), bf16[64,8,768]{2,1,0:T(8,128)(2,1)}, u32[]{:S(2)}, u32[]{:S(2)}) async-start(bf16[64,8,768]{2,1,0:T(8,128)(2,1)} %reshape.41), calls=%async_computation.7 | async-start | bytes 1572864 | tf_op jit(solution)/shard_map/all_to_all | solution.py:179
  212.6 0.9 copy-start.18
  213.6 0.9 copy-start.20
  215.1 0.8 copy-start.6
  215.9 1.4 copy-start.4
  217.3 1.4 copy-start.5
  218.7 1.0 copy-start.7
  236.5 15.3 %all-to-all-start.5 = ((bf16[4,4,3,64,128]{4,3,2,1,0:T(8,128)(2,1)}), bf16[4,4,3,64,128]{4,3,2,1,0:T(8,128)(2,1)S(1)}, u32[]{:S(2)}, u32[]{:S(2)}) async-start(bf16[4,4,3,64,128]{4,3,2,1,0:T(8,128)(2,1)} %pad_maximum_fusion), calls=%async_computation.5 | async-start | bytes 1572864 | tf_op jit(solution)/shard_map/all_to_all | solution.py:179
Sparse Core Ops, SparseCore 0:
  88.4 48.4 all-gather.4
  147.9 41.7 all-gather.6

commit v2 on v1

--- a/solution.py
+++ b/solution.py
@@ -27,17 +27,18 @@
 f32 = jnp.float32
 
 
-def call(body, out_shape, *args, flops=10**8):
+def call(body, out_shape, *args, scratch=(), alias=None, inside=True, flops=10**7):
     many = isinstance(out_shape, (list, tuple))
     outs = out_shape if many else [out_shape]
     nbytes = sum(math.prod(a.shape) * a.dtype.itemsize for a in list(args) + list(outs))
+    spec = pl.BlockSpec(memory_space=pltpu.VMEM) if inside else pl.BlockSpec()
     return pl.pallas_call(
         body,
         out_shape=out_shape,
-        in_specs=[pl.BlockSpec(memory_space=pltpu.VMEM)] * len(args),
-        out_specs=[pl.BlockSpec(memory_space=pltpu.VMEM)] * len(outs)
-        if many
-        else pl.BlockSpec(memory_space=pltpu.VMEM),
+        in_specs=[spec] * len(args),
+        out_specs=[spec] * len(outs) if many else spec,
+        scratch_shapes=list(scratch),
+        input_output_aliases=alias or {},
         compiler_params=pltpu.CompilerParams(vmem_limit_bytes=40 * 2**20),
         cost_estimate=pl.CostEstimate(flops=flops, bytes_accessed=nbytes, transcendentals=0),
     )(*args)
@@ -121,31 +122,47 @@
                 out[s, n, h] = res[:, s * 2 * DH : (s + 1) * 2 * DH]
 
 
-def key_side_kernel(by_query, queries, grads, out):
+def key_side_kernel(by_query, queries_grads, half, out):
+    del half
     for h in range(HL):
         lhs = jnp.concatenate(
             [by_query[r, h * CB : (h + 1) * CB, :] for r in range(NRES)], axis=0
         )
-        for n, (ref, low) in enumerate(((queries, CB), (grads, 0))):
+        for n, low in ((0, CB), (1, 0)):
             rhs = jnp.concatenate(
                 [
-                    jnp.concatenate([ref[r, s, h] for s in range(NHG)], axis=1)
+                    jnp.concatenate([queries_grads[r, s, n, h] for s in range(NHG)], axis=1)
                     for r in range(NRES)
                 ],
                 axis=0,
             )
             res = dot(lhs, rhs, 0, 0)[low : low + CB].astype(bf)
             for s in range(NHG):
-                out[s, n, h] = res[:, s * 2 * DH : (s + 1) * 2 * DH]
-
-
-def column_kernel(query, keys, values, grads, out):
+                out[s, 2 + n, h] = res[:, s * 2 * DH : (s + 1) * 2 * DH]
+
+
+def by_column_kernel(query, keys, values, grads, out, rows):
+    for pair in range(H // 2):
+        at = slice(pair * 2 * DH, (pair + 1) * 2 * DH)
+        for n, ref in enumerate((query, keys, values, grads)):
+            for r in range(2):
+                rows[pair, pl.ds(2 * n + r, CB, stride=8), :] = ref[r, :, at].astype(f32)
+        out[:, at] = rows[pair].astype(bf)
+
+
+def column_kernel(got, out, rows):
     lane = lax.broadcasted_iota(jnp.int32, (ROWS, 2 * DH), 1)
     first = lane < DH
     zero = jnp.zeros((ROWS, 2 * DH), bf)
     for pair in range(H // 2):
         at = slice(pair * 2 * DH, (pair + 1) * 2 * DH)
-        q, k, v, g = (ref[:, at] for ref in (query, keys, values, grads))
+        rows[pair] = got[:, at].astype(f32)
+        q, k, v, g = (
+            jnp.concatenate(
+                [rows[pair, pl.ds(2 * n + r, CB, stride=8), :] for r in range(2)], axis=0
+            ).astype(bf)
+            for n in range(4)
+        )
         res = []
         for half in range(2):
             keep = first if half == 0 else jnp.logical_not(first)
@@ -158,18 +175,30 @@
             db = dl.astype(bf)
             res.append((dot(pb, v, 1, 0), dot(db, k, 1, 0), dot(db, q, 0, 0), dot(pb, g, 0, 0)))
         for n in range(4):
-            out[n, :, at] = jnp.where(first, res[0][n], res[1][n]).astype(bf)
-
-
-def finish_kernel(rows, col_out, update, grad_q, grad_k, grad_v):
-    for pair in range(H // 2):
-        for n, ref in enumerate((update, grad_q, grad_k, grad_v)):
-            a, b = (rows[h // HL, n, h % HL] for h in (2 * pair, 2 * pair + 1))
+            both = jnp.where(first, res[0][n], res[1][n])
+            for r in range(2):
+                rows[pair, pl.ds(2 * n + r, CB, stride=8), :] = both[r * CB : (r + 1) * CB]
+        out[:, at] = rows[pair].astype(bf)
+
+
+def column_finish_kernel(columns, col_out, grad_cq, grad_ck, grad_cv, rows):
+    for pair in range(H // 2):
+        at = slice(pair * 2 * DH, (pair + 1) * 2 * DH)
+        rows[pair] = columns[:, at].astype(f32)
+        for n, ref in enumerate((col_out, grad_cq, grad_ck, grad_cv)):
+            for r in range(2):
+                ref[r, :, at] = rows[pair, pl.ds(2 * n + r, CB, stride=8), :].astype(bf)
+
+
+def finish_kernel(heads, col_out, update, grad_rq, grad_rk, grad_rv):
+    for pair in range(H // 2):
+        at = slice(pair * 2 * DH, (pair + 1) * 2 * DH)
+        for n, ref in enumerate((update, grad_rq, grad_rk, grad_rv)):
+            a, b = (heads[h // HL, n, h % HL] for h in (2 * pair, 2 * pair + 1))
             for r in range(2):
                 got = jnp.concatenate(
                     [a[:, r * DH : (r + 1) * DH], b[:, r * DH : (r + 1) * DH]], axis=1
                 )
-                at = slice(pair * 2 * DH, (pair + 1) * 2 * DH)
                 if n == 0:
                     got = (got.astype(f32) + col_out[r, :, at].astype(f32)).astype(bf)
                 ref[r, :, at] = got
@@ -181,23 +210,37 @@
 
 def on_device(row_q, row_k, row_v, col_q, col_k, col_v, cotangent):
     dev = sds((2, CB, H * DH), bf)
+    flat = sds((CB * 8, H * DH), bf)
+    room = pltpu.VMEM((H // 2, CB * 8, 2 * DH), f32)
     by_head = call(
-        to_heads_kernel, sds((NHG, 4, HL, CB, 2 * DH), bf), row_k, row_v, row_q, cotangent
+        to_heads_kernel,
+        sds((NHG, 4, HL, CB, 2 * DH), bf),
+        row_k,
+        row_v,
+        row_q,
+        cotangent,
+        inside=False,
     )
     mine = swap(by_head, HG)
-    queries = lax.all_gather(mine[:, 2], RES, axis=0)
-    grads = lax.all_gather(mine[:, 3], RES, axis=0)
-    own_kv = mine[:, :2]
-    keys_values = swap(jnp.broadcast_to(own_kv, (NRES,) + own_kv.shape), RES)
-
-    cols = jnp.stack([col_q, col_k, col_v, cotangent]).transpose(2, 0, 1, 3)
-    cols = swap(cols.reshape(CB, 8, H * DH), DEP)
-    cols = cols.reshape(CB, 4, 2, H * DH).transpose(1, 0, 2, 3).reshape(4, ROWS, H * DH)
+    keys_values = lax.all_gather(mine[:, :2], RES, axis=0)
+    queries_grads = lax.all_gather(mine[:, 2:], RES, axis=0)
+
+    cols = call(
+        by_column_kernel, flat, col_q, col_k, col_v, cotangent, scratch=[room], inside=False
+    )
+    cols, mine = lax.optimization_barrier((cols, mine))
+    cols = swap(cols, DEP)
+    cols = call(column_kernel, flat, cols, scratch=[room], flops=10**9)
+    cols = swap(cols, DEP)
+    cols, mine = lax.optimization_barrier((cols, mine))
 
     parts = call(logits_kernel, sds((NRED, 2 * QR, COLS), f32), mine, keys_values)
     parts = swap(parts, RED)
     rows = call(softmax_kernel, sds((NRED, 2 * QR, COLS), bf), parts)
     rows = swap(rows, RED)
+    col_out, grad_cq, grad_ck, grad_cv = call(
+        column_finish_kernel, [dev] * 4, cols, scratch=[room], inside=False
+    )
     probs, dlogits, by_key = call(
         assemble_kernel,
         [
@@ -208,18 +251,14 @@
         rows,
     )
     by_query = swap(by_key, RES)
-    side = sds((NHG, 2, HL, CB, 2 * DH), bf)
-    query_side = call(query_side_kernel, side, probs, dlogits, keys_values)
-
-    done = call(column_kernel, sds((4, ROWS, H * DH), bf), cols[0], cols[1], cols[2], cols[3])
-    done = done.reshape(4, CB, 2, H * DH).transpose(1, 0, 2, 3).reshape(CB, 8, H * DH)
-    done = swap(done, DEP)
-    done = done.reshape(CB, 4, 2, H * DH).transpose(1, 2, 0, 3)
-
-    key_side = call(key_side_kernel, side, by_query, queries, grads)
-    back = swap(jnp.concatenate([query_side, key_side], axis=1), HG)
-    update, grad_rq, grad_rk, grad_rv = call(finish_kernel, [dev] * 4, back, done[0])
-    return update, grad_rq, grad_rk, grad_rv, done[1], done[2], done[3]
+    back = sds((NHG, 4, HL, CB, 2 * DH), bf)
+    half = call(query_side_kernel, back, probs, dlogits, keys_values)
+    back = call(key_side_kernel, back, by_query, queries_grads, half, alias={2: 0})
+    back = swap(back, HG)
+    update, grad_rq, grad_rk, grad_rv = call(
+        finish_kernel, [dev] * 4, back, col_out, inside=False
+    )
+    return update, grad_rq, grad_rk, grad_rv, grad_cq, grad_ck, grad_cv
 
 
 def solution(mesh):

time: 262 us -> 218 us (0.83)
  blocking collectives: 59.3 us -> 106 us
  local copies, waits for them, and re-layouts: 47.3 us -> 15.4 us
  starting transfers between devices: 50.6 us -> 22.5 us
  waiting for transfers between devices: 75.1 us -> 47.2 us
    all_to_all x2 -> x4, blocking collectives: 59.3 us -> 106 us  [swap(): return lax.all_to_all(array, axes, 0, 0, tiled=True)]
    all_to_all x6 -> x3, waiting for transfers between devices: 74.3 us -> 36.3 us  [swap(): return lax.all_to_all(array, axes, 0, 0, tiled=True)]
    all_to_all x6 -> x3, starting transfers between devices: 50.5 us -> 22.4 us  [swap(): return lax.all_to_all(array, axes, 0, 0, tiled=True)]
    all_gather x2, waiting for transfers between devices: 0.01 us -> 10.1 us  [the longest x1 6.6 us: on_device(): keys_values = lax.all_gather(mine[:, :2], RES, axis=0)]
    slice x7 -> x1, local copies, waits for them, and re-layouts: 8.93 us -> 1 us  [on_device(): queries_grads = lax.all_gather(mine[:, 2:], RES, axis=0)]
    squeeze x5 -> x0, local copies, waits for them, and re-layouts: 7.53 us -> none  [the longest x1 1.68 us: on_device(): cols[3]]
    reshape x3 -> x0, local copies, waits for them, and re-layouts: 7.11 us -> none  [the longest x2 5.81 us: on_device(): done.reshape(4, CB, 2, H * DH).transpose(1, 0, 2, 3).reshape(CB, 8, H * DH)]
    unnamed x42 -> x40, local copies, waits for them, and re-layouts: 17.9 us -> 14.4 us
  transfers between devices with their start and end apart: 8 -> 5, of which waited for: 5 -> 5; matrix products, arithmetic and copies ran while one was open for 12% -> 0% of each run, Pallas kernels for 3% -> 5%
where the time goes in v2:
time: 218 us; the launch traced here: 217 us
  blocking collectives  106 us (49%)
  waiting for transfers between devices  47.2 us (22%)
  starting transfers between devices  22.5 us (10%)
  local copies, waits for them, and re-layouts  15.4 us (7%)
  between operations  14.2 us (7%)
  Pallas kernels  12.3 us (6%)
    all_to_all x4, blocking collectives, swap(): return lax.all_to_all(array, axes, 0, 0, tiled=True)  106 us
    all_to_all x3, waiting for transfers between devices, swap(): return lax.all_to_all(array, axes, 0, 0, tiled=True)  36.3 us
    all_to_all x3, starting transfers between devices, swap(): return lax.all_to_all(array, axes, 0, 0, tiled=True)  22.4 us
    unnamed x40, local copies, waits for them, and re-layouts  14.4 us
    pallas_call x10, Pallas kernels, call(): pl.pallas_call(body, out_shape=out_shape, in_specs=[spec] * len(args), ou...  12.3 us
    all_gather x1, waiting for transfers between devices, on_device(): keys_values = lax.all_gather(mine[:, :2], RES, axis=0)  6.6 us
  transfers between devices with their start and end apart: 5, of which 5 were waited for; matrix products, arithmetic and copies ran while one was open for 0% of the time, Pallas kernels for 5%

profile of v2, /device:TPU:1, one launch (start us, length us, event | category | flops | bytes accessed | tf_op | source)
XLA Modules:
  0.0 217.4 jit_solution(5903949536663140)
XLA Ops:
  7.2 0.9 copy-done.7
  8.1 0.9 copy-done.14
  9.1 0.9 copy-done.15
  10.0 0.9 copy-done.16
  11.2 20.0 %all_to_all.48.mine = bf16[4,4,3,64,128]{4,3,2,1,0:T(8,128)(2,1)S(1)} all-to-all(bf16[4,4,3,64,128]{4,3,2,1,0:T(8,128)(2,1)S(1)} %shard_map.127), channel_id=1, replica_groups=mesh['yhi'=4,'ylo'=2,'zhi'=4,'core'=2,'zlo'=2,'x'=4] {'ylo','core'}, dimensions={0} | all-to-all | bytes 1572864 | tf_op jit(solution)/shard_map/all_to_all | solution.py:208
  31.2 1.0 fusion
  32.3 1.3 shard_map.126
  33.6 11.8 %all-to-all-start.1 = ((bf16[64,8,768]{2,1,0:T(8,128)(2,1)}), bf16[64,8,768]{2,1,0:T(8,128)(2,1)S(1)}, u32[]{:S(2)}, u32[]{:S(2)}) async-start(bf16[64,8,768]{2,1,0:T(8,128)(2,1)} %bitcast), calls=%async_computation.1 | async-start | bytes 1572864 | tf_op jit(solution)/shard_map/all_to_all | solution.py:208
  45.5 0.7 all-gather.7.cloned.1.call-update
  46.2 23.2 %all-to-all-done.1 = bf16[64,8,768]{2,1,0:T(8,128)(2,1)S(1)} async-done(((bf16[64,8,768]{2,1,0:T(8,128)(2,1)}), bf16[64,8,768]{2,1,0:T(8,128)(2,1)S(1)}, u32[]{:S(2)}, u32[]{:S(2)}) %all-to-all-start.1) | async-done | bytes 786464 | tf_op jit(solution)/shard_map/all_to_all | solution.py:208
  69.4 5.7 %shard_map.128 = bf16[512,768]{1,0:T(8,128)(2,1)S(1)} custom-call(bf16[512,768]{1,0:T(8,128)(2,1)S(1)} %bitcast.10), custom_call_target="tpu_custom_call" | custom-call | flops 1000000000 | bytes 1572864 | tf_op jit(solution)/shard_map/pallas_call | solution.py:35
  75.1 31.7 %all_to_all.49 = bf16[64,8,768]{2,1,0:T(8,128)(2,1)} all-to-all(bf16[64,8,768]{2,1,0:T(8,128)(2,1)S(1)} %bitcast.11), channel_id=1, replica_groups=mesh['yhi'=4,'ylo'=2,'zhi'=4,'core'=2,'zlo'=2,'x'=4] {'yhi','ylo','zhi',..., dimensions={0} | all-to-all | bytes 1572864 | tf_op jit(solution)/shard_map/all_to_all | solution.py:208
  106.8 6.6 %all-gather.5.cloned.1.call-done = bf16[32,2,3,64,128]{4,3,2,1,0:T(8,128)(2,1)} async-done(((bf16[4,2,3,64,128]{4,3,2,1,0:T(8,128)(2,1)}), bf16[32,2,3,64,128]{4,3,2,1,0:T(8,128)(2,1)}) %all-gather.5.cloned.1.call-update) | async-done | bytes 3145744 | tf_op jit(solution)/shard_map/all_gather | solution.py:225
  113.4 1.9 copy-done
  115.2 1.1 shard_map.129
  116.3 35.6 %all_to_all.50.parts = f32[16,24,512]{2,1,0:T(8,128)S(1)} all-to-all(f32[16,24,512]{2,1,0:T(8,128)S(1)} %shard_map.129), channel_id=1, replica_groups=mesh['yhi'=4,'ylo'=2,'zhi'=4,'core'=2,'zlo'=2,'x'=4] {'yhi','zhi'}, dimensions={0} | all-to-all | bytes 1572864 | tf_op jit(solution)/shard_map/all_to_all | solution.py:208
  152.2 18.6 %all_to_all.51.rows = bf16[16,24,512]{2,1,0:T(8,128)(2,1)S(1)} all-to-all(bf16[16,24,512]{2,1,0:T(8,128)(2,1)S(1)} %shard_map.130), channel_id=1, replica_groups=mesh['yhi'=4,'ylo'=2,'zhi'=4,'core'=2,'zlo'=2,'x'=4] {'yhi','zhi'}, dimensions={0} | all-to-all | bytes 786432 | tf_op jit(solution)/shard_map/all_to_all | solution.py:208
  171.0 0.8 copy-done.9
  171.8 0.7 copy-done.10
  173.2 6.7 %all-to-all-start.5 = ((bf16[8,192,128]{2,1,0:T(8,128)(2,1)}), bf16[8,192,128]{2,1,0:T(8,128)(2,1)S(1)}, u32[]{:S(2)}, u32[]{:S(2)}) async-start(bf16[8,192,128]{2,1,0:T(8,128)(2,1)} %copy-done.9), calls=%async_computation.5 | async-start | bytes 786432 | tf_op jit(solution)/shard_map/all_to_all | solution.py:208
  179.8 0.9 copy-done.11
  180.8 0.9 copy-done.13
  182.3 0.9 copy-done.2
  183.2 3.5 %all-gather.7.cloned.1.call-done = bf16[32,2,3,64,128]{4,3,2,1,0:T(8,128)(2,1)} async-done(((bf16[4,2,3,64,128]{4,3,2,1,0:T(8,128)(2,1)}), bf16[32,2,3,64,128]{4,3,2,1,0:T(8,128)(2,1)}) %all-gather.7.cloned.1.call-update) | async-done | bytes 3145744 | tf_op jit(solution)/shard_map/all_gather | solution.py:226
  186.7 3.5 %all-to-all-done.5.by_query = bf16[8,192,128]{2,1,0:T(8,128)(2,1)S(1)} async-done(((bf16[8,192,128]{2,1,0:T(8,128)(2,1)}), bf16[8,192,128]{2,1,0:T(8,128)(2,1)S(1)}, u32[]{:S(2)}, u32[]{:S(2)}) %all-to-all-start.5) | async-done | bytes 393248 | tf_op jit(solution)/shard_map/all_to_all | solution.py:208
  190.2 1.1 copy-done.3
  191.3 1.9 copy-done.5
  193.8 0.9 copy-done.4
  194.7 4.0 %all-to-all-start.6 = ((bf16[4,4,3,64,128]{4,3,2,1,0:T(8,128)(2,1)}), bf16[4,4,3,64,128]{4,3,2,1,0:T(8,128)(2,1)S(1)}, u32[]{:S(2)}, u32[]{:S(2)}) async-start(bf16[4,4,3,64,128]{4,3,2,1,0:T(8,128)(2,1)} %copy-done.4), calls=%async_computation.6 | async-start | bytes 1572864 | tf_op jit(solution)/shard_map/all_to_all | solution.py:208
  198.7 1.1 shard_map.134
  199.8 9.7 %all-to-all-done.6.heads = bf16[4,4,3,64,128]{4,3,2,1,0:T(8,128)(2,1)S(1)} async-done(((bf16[4,4,3,64,128]{4,3,2,1,0:T(8,128)(2,1)}), bf16[4,4,3,64,128]{4,3,2,1,0:T(8,128)(2,1)S(1)}, u32[]{:S(2)}, u32[]{:S(2)}) %all-to-all-start.6) | async-done | bytes 786464 | tf_op jit(solution)/shard_map/all_to_all | solution.py:208
  209.5 1.1 shard_map.135
  (35 shorter events, 2.8 us)
Async XLA Ops:
  7.2 106.2 %all-gather.5.cloned.1.call-start = ((), (), s32[]{:S(2)}) async-start(), calls=%async_computation.7 | async-start | bytes 3538944 | tf_op jit(solution)/shard_map/all_gather | solution.py:225
  7.2 0.9 copy-start.7
  8.1 0.9 copy-start.14
  9.1 0.9 copy-start.15
  10.0 0.9 copy-start.16
  10.9 21.4 %copy-start.8 = (bf16[2,64,768]{2,1,0:T(8,128)(2,1)S(1)}, bf16[2,64,768]{2,1,0:T(8,128)(2,1)}, u32[]{:S(2)}) copy-start(bf16[2,64,768]{2,1,0:T(8,128)(2,1)} %refs_3_.1) | copy-start | bytes 589828
  10.9 21.4 %copy-start.17 = (bf16[2,64,768]{2,1,0:T(8,128)(2,1)S(1)}, bf16[2,64,768]{2,1,0:T(8,128)(2,1)}, u32[]{:S(2)}) copy-start(bf16[2,64,768]{2,1,0:T(8,128)(2,1)} %query.1) | copy-start | bytes 589828
  10.9 21.4 %copy-start.18 = (bf16[2,64,768]{2,1,0:T(8,128)(2,1)S(1)}, bf16[2,64,768]{2,1,0:T(8,128)(2,1)}, u32[]{:S(2)}) copy-start(bf16[2,64,768]{2,1,0:T(8,128)(2,1)} %keys.1) | copy-start | bytes 589828
  10.9 21.4 %copy-start.19 = (bf16[2,64,768]{2,1,0:T(8,128)(2,1)S(1)}, bf16[2,64,768]{2,1,0:T(8,128)(2,1)}, u32[]{:S(2)}) copy-start(bf16[2,64,768]{2,1,0:T(8,128)(2,1)} %values.1) | copy-start | bytes 589828
  33.6 35.7 %all-to-all-start.1 = ((bf16[64,8,768]{2,1,0:T(8,128)(2,1)}), bf16[64,8,768]{2,1,0:T(8,128)(2,1)S(1)}, u32[]{:S(2)}, u32[]{:S(2)}) async-start(bf16[64,8,768]{2,1,0:T(8,128)(2,1)} %bitcast), calls=%async_computation.1 | async-start | bytes 1572864 | tf_op jit(solution)/shard_map/all_to_all | solution.py:208
  45.4 141.3 %all-gather.7.cloned.1.call-start = ((), (), s32[]{:S(2)}) async-start(), calls=%async_computation.8 | async-start | bytes 3538944 | tf_op jit(solution)/shard_map/all_gather | solution.py:226
  113.4 1.9 copy-start
  116.3 63.5 %copy-start.1 = (bf16[32,2,3,64,128]{4,3,2,1,0:T(8,128)(2,1)S(1)}, bf16[32,2,3,64,128]{4,3,2,1,0:T(8,128)(2,1)}, u32[]{:S(2)}) copy-start(bf16[32,2,3,64,128]{4,3,2,1,0:T(8,128)(2,1)} %all-gather.5.cloned.1.call-done) | copy-start | bytes 9437188
  171.0 0.8 copy-start.9
  171.8 0.7 copy-start.10
  172.5 0.7 copy-start.12
  173.2 17.0 %all-to-all-start.5 = ((bf16[8,192,128]{2,1,0:T(8,128)(2,1)}), bf16[8,192,128]{2,1,0:T(8,128)(2,1)S(1)}, u32[]{:S(2)}, u32[]{:S(2)}) async-start(bf16[8,192,128]{2,1,0:T(8,128)(2,1)} %copy-done.9), calls=%async_computation.5 | async-start | bytes 786432 | tf_op jit(solution)/shard_map/all_to_all | solution.py:208
  179.8 0.9 copy-start.11
  180.8 0.9 copy-start.13
  182.3 0.9 copy-start.2
  190.2 1.1 copy-start.3
  191.3 1.9 copy-start.5
  193.2 5.5 %copy-start.6 = (bf16[64,8,768]{2,1,0:T(8,128)(2,1)S(1)}, bf16[64,8,768]{2,1,0:T(8,128)(2,1)}, u32[]{:S(2)}) copy-start(bf16[64,8,768]{2,1,0:T(8,128)(2,1)} %all_to_all.49) | copy-start | bytes 2359300
  193.8 0.9 copy-start.4
  194.7 14.8 %all-to-all-start.6 = ((bf16[4,4,3,64,128]{4,3,2,1,0:T(8,128)(2,1)}), bf16[4,4,3,64,128]{4,3,2,1,0:T(8,128)(2,1)S(1)}, u32[]{:S(2)}, u32[]{:S(2)}) async-start(bf16[4,4,3,64,128]{4,3,2,1,0:T(8,128)(2,1)} %copy-done.4), calls=%async_computation.6 | async-start | bytes 1572864 | tf_op jit(solution)/shard_map/all_to_all | solution.py:208
Sparse Core Ops, SparseCore 0:
  32.4 80.9 all-gather.4
  115.4 71.2 all-gather.6

commit v3 on v2

v3 whole, which is shorter than its diff:
```python
import math

import jax
import jax.numpy as jnp
from jax import lax
from jax.experimental import pallas as pl
from jax.experimental.pallas import tpu as pltpu
from jax.sharding import Mesh, PartitionSpec as P

H = 12
DH = 64
ROWS = 128
COLS = 512
HG = ("ylo", "core")
HGZ = ("ylo", "core", "zlo")
RED = ("yhi", "zhi")
DEP = ("yhi", "ylo", "zhi", "core")
RES = ("zlo", "x")
NHG = 4
HL = 3
NRED = 16
NRES = 8
NX = 4
NZ = 2
CB = 64
QR = HL * CB // NRED
ROW_SCALE = 1.0 / math.sqrt(DH) / math.sqrt(ROWS)
COL_SCALE = 1.0 / math.sqrt(DH)
bf = jnp.bfloat16
f32 = jnp.float32


def call(body, out_shape, *args, scratch=(), inside=True, flops=10**7):
    many = isinstance(out_shape, (list, tuple))
    outs = out_shape if many else [out_shape]
    nbytes = sum(math.prod(a.shape) * a.dtype.itemsize for a in list(args) + list(outs))
    spec = pl.BlockSpec(memory_space=pltpu.VMEM) if inside else pl.BlockSpec()
    return pl.pallas_call(
        body,
        out_shape=out_shape,
        in_specs=[spec] * len(args),
        out_specs=[spec] * len(outs) if many else spec,
        scratch_shapes=list(scratch),
        compiler_params=pltpu.CompilerParams(vmem_limit_bytes=(24 if inside else 56) * 2**20),
        cost_estimate=pl.CostEstimate(flops=flops, bytes_accessed=nbytes, transcendentals=0),
    )(*args)


def sds(shape, dtype):
    return jax.ShapeDtypeStruct(shape, dtype)


def dot(a, b, ca, cb):
    return lax.dot_general(a, b, (((ca,), (cb,)), ((), ())), preferred_element_type=f32)


def to_heads_kernel(*refs):
    out = refs[-1]
    for n, ref in enumerate(refs[:-1]):
        for h in range(H):
            a = ref[0, :, h * DH : (h + 1) * DH]
            b = ref[1, :, h * DH : (h + 1) * DH]
            both = jnp.concatenate([a, b], axis=1)
            for z in range(NZ):
                out[h // HL, z, n, h % HL] = both


def gathered(ref, n, h):
    return jnp.concatenate(
        [
            jnp.concatenate([ref[x, s, z, n, h] for s in range(NHG)], axis=1)
            for z in range(NZ)
            for x in range(NX)
        ],
        axis=0,
    )


def logits_kernel(mine, keys_values, out):
    own = lax.axis_index("zlo")
    logits, dprobs = [], []
    for h in range(HL):
        for res, n, which in ((logits, 0, 0), (dprobs, 1, 1)):
            lhs = jnp.concatenate([mine[s, own, n, h] for s in range(NHG)], axis=1)
            res.append(dot(lhs, gathered(keys_values, which, h), 1, 1))
    logits = jnp.concatenate(logits, axis=0)
    dprobs = jnp.concatenate(dprobs, axis=0)
    dprobs = dprobs - jnp.mean(dprobs, axis=-1, keepdims=True)
    high = logits.astype(bf).astype(f32)
    rest = logits - high
    for m in range(NRED):
        at = slice(m * QR, (m + 1) * QR)
        out[m] = jnp.concatenate([high[at], rest[at], dprobs[at]], axis=0).astype(bf)


def softmax_kernel(parts, out):
    total = parts[0].astype(f32)
    for m in range(1, NRED):
        total = total + parts[m].astype(f32)
    logits = (total[:QR] + total[QR : 2 * QR]) * ROW_SCALE
    dprobs = total[2 * QR :]
    e = jnp.exp(logits - jnp.max(logits, axis=-1, keepdims=True))
    probs = e / jnp.sum(e, axis=-1, keepdims=True)
    dl = probs * (dprobs - jnp.sum(probs * dprobs, axis=-1, keepdims=True)) * ROW_SCALE
    both = jnp.concatenate([probs, dl], axis=0).astype(bf)
    for m in range(NRED):
        out[m] = both


def assemble_kernel(rows, probs, dlogits, by_key):
    parts = [rows[m].astype(f32) for m in range(NRED)]
    p = jnp.concatenate([a[:QR] for a in parts], axis=0).astype(bf)
    d = jnp.concatenate([a[QR:] for a in parts], axis=0).astype(bf)
    probs[...] = p
    dlogits[...] = d
    for r in range(NRES):
        by_key[r] = jnp.concatenate(
            [p[:, r * CB : (r + 1) * CB], d[:, r * CB : (r + 1) * CB]], axis=1
        )


def row_grads_kernel(probs, dlogits, by_query, keys_values, queries_grads, out):

    def put(n, h, res):
        for s in range(NHG):
            out[s, n, h] = res[:, s * 2 * DH : (s + 1) * 2 * DH].astype(bf)

    for h in range(HL):
        at = slice(h * CB, (h + 1) * CB)
        put(0, h, dot(probs[at, :], gathered(keys_values, 1, h), 1, 0))
        put(1, h, dot(dlogits[at, :], gathered(keys_values, 0, h), 1, 0))
        lhs = jnp.concatenate([by_query[r, at, :] for r in range(NRES)], axis=0)
        put(2, h, dot(lhs, gathered(queries_grads, 0, h), 0, 0)[CB:])
        put(3, h, dot(lhs, gathered(queries_grads, 1, h), 0, 0)[:CB])


def by_column_kernel(query, keys, values, grads, out, rows):
    for pair in range(H // 2):
        at = slice(pair * 2 * DH, (pair + 1) * 2 * DH)
        for n, ref in enumerate((query, keys, values, grads)):
            for r in range(2):
                rows[pair, pl.ds(2 * n + r, CB, stride=8), :] = ref[r, :, at].astype(f32)
        out[:, at] = rows[pair].astype(bf)


def column_kernel(got, out, rows):
    low = lax.broadcasted_iota(jnp.int32, (ROWS, 2 * DH), 1) < DH
    zero = jnp.zeros((ROWS, 2 * DH), bf)

    def stacked(x):
        return jnp.concatenate([jnp.where(low, x, zero), jnp.where(low, zero, x)], axis=0)

    def beside(x):
        return jnp.concatenate([x[:ROWS], x[ROWS:]], axis=1)

    for pair in range(H // 2):
        at = slice(pair * 2 * DH, (pair + 1) * 2 * DH)
        rows[pair] = got[:, at].astype(f32)
        q, k, v, g = (
            jnp.concatenate(
                [rows[pair, pl.ds(2 * n + r, CB, stride=8), :] for r in range(2)], axis=0
            ).astype(bf)
            for n in range(4)
        )
        qs, ks, vs, gs = (stacked(x) for x in (q, k, v, g))
        logits = dot(qs, k, 1, 1) * COL_SCALE
        dprobs = dot(gs, v, 1, 1)
        e = jnp.exp(logits - jnp.max(logits, axis=-1, keepdims=True))
        probs = e / jnp.sum(e, axis=-1, keepdims=True)
        dl = probs * (dprobs - jnp.sum(probs * dprobs, axis=-1, keepdims=True)) * COL_SCALE
        pb = probs.astype(bf)
        db = dl.astype(bf)
        res = (
            dot(beside(pb), vs, 1, 0),
            dot(beside(db), ks, 1, 0),
            dot(db, qs, 0, 0),
            dot(pb, gs, 0, 0),
        )
        for n in range(4):
            for r in range(2):
                rows[pair, pl.ds(2 * n + r, CB, stride=8), :] = res[n][r * CB : (r + 1) * CB]
        out[:, at] = rows[pair].astype(bf)


def column_finish_kernel(columns, col_out, grad_cq, grad_ck, grad_cv, rows):
    for pair in range(H // 2):
        at = slice(pair * 2 * DH, (pair + 1) * 2 * DH)
        rows[pair] = columns[:, at].astype(f32)
        for n, ref in enumerate((col_out, grad_cq, grad_ck, grad_cv)):
            for r in range(2):
                ref[r, :, at] = rows[pair, pl.ds(2 * n + r, CB, stride=8), :].astype(bf)


def finish_kernel(heads, col_out, update, grad_rq, grad_rk, grad_rv):
    for pair in range(H // 2):
        at = slice(pair * 2 * DH, (pair + 1) * 2 * DH)
        for n, ref in enumerate((update, grad_rq, grad_rk, grad_rv)):
            a, b = (heads[h // HL, n, h % HL] for h in (2 * pair, 2 * pair + 1))
            for r in range(2):
                got = jnp.concatenate(
                    [a[:, r * DH : (r + 1) * DH], b[:, r * DH : (r + 1) * DH]], axis=1
                )
                if n == 0:
                    got = (got.astype(f32) + col_out[r, :, at].astype(f32)).astype(bf)
                ref[r, :, at] = got


def swap(array, axes):
    return lax.all_to_all(array, axes, 0, 0, tiled=True)


def on_device(row_q, row_k, row_v, col_q, col_k, col_v, cotangent):
    dev = sds((2, CB, H * DH), bf)
    flat = sds((CB * 8, H * DH), bf)
    room = pltpu.VMEM((H // 2, CB * 8, 2 * DH), f32)
    by_head = call(
        to_heads_kernel,
        sds((NHG, NZ, 4, HL, CB, 2 * DH), bf),
        row_k,
        row_v,
        row_q,
        cotangent,
        inside=False,
    )
    mine = swap(by_head.reshape((NHG * NZ,) + by_head.shape[2:]), HGZ).reshape(by_head.shape)
    keys_values, mine = mine[:, :, :2], mine[:, :, 2:]
    keys_values = lax.all_gather(keys_values, "x", axis=0)
    queries_grads = lax.all_gather(mine, "x", axis=0)

    cols = call(
        by_column_kernel, flat, col_q, col_k, col_v, cotangent, scratch=[room]
    )
    cols, mine = lax.optimization_barrier((cols, mine))
    cols = swap(cols, DEP)
    cols = call(column_kernel, flat, cols, scratch=[room], flops=10**9)
    cols = swap(cols, DEP)
    cols, mine = lax.optimization_barrier((cols, mine))

    parts = call(
        logits_kernel,
        sds((NRED, 3 * QR, COLS), bf),
        mine,
        keys_values,
    )
    parts = swap(parts, RED)
    rows = call(softmax_kernel, sds((NRED, 2 * QR, COLS), bf), parts)
    rows = swap(rows, RED)
    col_out, grad_cq, grad_ck, grad_cv = call(
        column_finish_kernel, [dev] * 4, cols, scratch=[room], inside=False
    )
    rows, queries_grads, col_out = lax.optimization_barrier((rows, queries_grads, col_out))
    probs, dlogits, by_key = call(
        assemble_kernel,
        [
            sds((HL * CB, COLS), bf),
            sds((HL * CB, COLS), bf),
            sds((NRES, HL * CB, 2 * CB), bf),
        ],
        rows,
    )
    by_query = swap(by_key, RES)
    back = call(
        row_grads_kernel,
        sds((NHG, 4, HL, CB, 2 * DH), bf),
        probs,
        dlogits,
        by_query,
        keys_values,
        queries_grads,
    )
    back = swap(back, HG)
    update, grad_rq, grad_rk, grad_rv = call(
        finish_kernel, [dev] * 4, back, col_out, inside=False
    )
    return update, grad_rq, grad_rk, grad_rv, grad_cq, grad_ck, grad_cv


def solution(mesh):
    fine = Mesh(
        mesh.devices.reshape(4, 2, 4, 2, 2, 4), ("yhi", "ylo", "zhi", "core", "zlo", "x")
    )
    spec = P(DEP, RES, None)
    return jax.shard_map(
        on_device, mesh=fine, in_specs=(spec,) * 7, out_specs=(spec,) * 7, check_vma=False
    )
```

time: 218 us -> 209 us (0.959)
  blocking collectives: 106 us -> 120 us
  waiting for transfers between devices: 47.2 us -> 34.9 us
  local copies, waits for them, and re-layouts: 15.4 us -> 6.12 us
  starting transfers between devices: 22.5 us -> 18.5 us
  Pallas kernels: 12.3 us -> 14.6 us
    all_to_all x4 -> x5, blocking collectives: 106 us -> 120 us  [swap(): return lax.all_to_all(array, axes, 0, 0, tiled=True)]
    all_gather x2, waiting for transfers between devices: 10.1 us -> 0.01 us  [the longest x1 0.01 us: on_device(): keys_values = lax.all_gather(keys_values, 'x', axis=0)]
    unnamed x40 -> x18, local copies, waits for them, and re-layouts: 14.4 us -> 4.78 us
    all_to_all x3 -> x2, starting transfers between devices: 22.4 us -> 18.5 us  [swap(): return lax.all_to_all(array, axes, 0, 0, tiled=True)]
    pallas_call x10 -> x9, Pallas kernels: 12.3 us -> 14.6 us  [call(): pl.pallas_call(body, out_shape=out_shape, in_specs=[spec] * len(args), ou...]
    all_to_all x3 -> x2, waiting for transfers between devices: 36.3 us -> 34.2 us  [swap(): return lax.all_to_all(array, axes, 0, 0, tiled=True)]
  transfers between devices with their start and end apart: 5 -> 4, of which waited for: 5 -> 2; matrix products, arithmetic and copies ran while one was open for 0% -> 0% of each run, Pallas kernels for 5% -> 4%
where the time goes in v3:
time: 209 us; the launch traced here: 208 us
  blocking collectives  120 us (57%)
  waiting for transfers between devices  34.9 us (17%)
  starting transfers between devices  18.5 us (9%)
  Pallas kernels  14.6 us (7%)
  between operations  14.1 us (7%)
  local copies, waits for them, and re-layouts  6.12 us (3%)
    all_to_all x5, blocking collectives, swap(): return lax.all_to_all(array, axes, 0, 0, tiled=True)  120 us
    all_to_all x2, waiting for transfers between devices, swap(): return lax.all_to_all(array, axes, 0, 0, tiled=True)  34.2 us
    all_to_all x2, starting transfers between devices, swap(): return lax.all_to_all(array, axes, 0, 0, tiled=True)  18.5 us
    pallas_call x9, Pallas kernels, call(): pl.pallas_call(body, out_shape=out_shape, in_specs=[spec] * len(args), ou...  14.6 us
    unnamed x18, local copies, waits for them, and re-layouts  4.78 us
  transfers between devices with their start and end apart: 4, of which 2 were waited for; matrix products, arithmetic and copies ran while one was open for 0% of the time, Pallas kernels for 4%

profile of v3, /device:TPU:1, one launch (start us, length us, event | category | flops | bytes accessed | tf_op | source)
XLA Modules:
  0.0 208.3 jit_solution(16357451015992094307)
XLA Ops:
  7.2 0.0 all-gather.5.cloned.1.call-start
  7.2 2.7 %shard_map.127 = bf16[4,2,4,3,64,128]{5,4,3,2,1,0:T(8,128)(2,1)} custom-call(bf16[2,64,768]{2,1,0:T(8,128)(2,1)} %refs_0_.1, bf16[2,64,768]{2,1,0:T(8,128)(2,1)} %refs_1_.1, bf16[2,64,768]{2,1,0:T(8,128)(2,1)} %refs_2_.1, bf16[2,64,768]{2,1,0:T(8,128)(2,1)} %refs_3_.1), custom_call_target="tpu_custom_call" | custom-call | flops 10000000 | bytes 2359296 | tf_op jit(solution)/shard_map/pallas_call | solution.py:38
  9.9 30.3 %all_to_all.48 = bf16[8,4,3,64,128]{4,3,2,1,0:T(8,128)(2,1)S(1)} all-to-all(bf16[8,4,3,64,128]{4,3,2,1,0:T(8,128)(2,1)} %bitcast.14), channel_id=1, replica_groups=mesh['yhi'=4,'ylo'=2,'zhi'=4,'core'=2,'zlo'=2,'x'=4] {'ylo','core','zlo'}, dimensions={0} | all-to-all | bytes 3145728 | tf_op jit(solution)/shard_map/all_to_all | solution.py:209
  40.2 1.3 fusion
  41.5 0.0 all-gather.5.cloned.1.call-update
  41.5 0.0 copy-done.5
  41.6 0.0 copy-done.6
  41.6 0.0 copy-done.7
  41.6 0.2 copy-done.8
  41.8 1.4 shard_map.126
  43.2 10.9 %all-to-all-start.1 = ((bf16[64,8,768]{2,1,0:T(8,128)(2,1)}), bf16[64,8,768]{2,1,0:T(8,128)(2,1)S(1)}, u32[]{:S(2)}, u32[]{:S(2)}) async-start(bf16[64,8,768]{2,1,0:T(8,128)(2,1)} %bitcast.2), calls=%async_computation.1 | async-start | bytes 1572864 | tf_op jit(solution)/shard_map/all_to_all | solution.py:209
  54.1 0.0 all-gather.7.cloned.1.call-start
  54.1 0.7 all-gather.7.cloned.1.call-update
  54.8 23.2 %all-to-all-done.1 = bf16[64,8,768]{2,1,0:T(8,128)(2,1)S(1)} async-done(((bf16[64,8,768]{2,1,0:T(8,128)(2,1)}), bf16[64,8,768]{2,1,0:T(8,128)(2,1)S(1)}, u32[]{:S(2)}, u32[]{:S(2)}) %all-to-all-start.1) | async-done | bytes 786464 | tf_op jit(solution)/shard_map/all_to_all | solution.py:209
  78.0 3.1 %shard_map.128 = bf16[512,768]{1,0:T(8,128)(2,1)S(1)} custom-call(bf16[512,768]{1,0:T(8,128)(2,1)S(1)} %bitcast.11), custom_call_target="tpu_custom_call" | custom-call | flops 1000000000 | bytes 1572864 | tf_op jit(solution)/shard_map/pallas_call | solution.py:38
  81.2 31.0 %all_to_all.49 = bf16[64,8,768]{2,1,0:T(8,128)(2,1)} all-to-all(bf16[64,8,768]{2,1,0:T(8,128)(2,1)S(1)} %bitcast.12), channel_id=1, replica_groups=mesh['yhi'=4,'ylo'=2,'zhi'=4,'core'=2,'zlo'=2,'x'=4] {'yhi','ylo','zhi',..., dimensions={0} | all-to-all | bytes 1572864 | tf_op jit(solution)/shard_map/all_to_all | solution.py:209
  112.2 0.0 copy-done.2
  112.2 1.9 copy-done
  114.2 1.1 shard_map.129
  115.3 25.1 %all_to_all.50.parts = bf16[16,36,512]{2,1,0:T(8,128)(2,1)S(1)} all-to-all(bf16[16,36,512]{2,1,0:T(8,128)(2,1)S(1)} %shard_map.129), channel_id=1, replica_groups=mesh['yhi'=4,'ylo'=2,'zhi'=4,'core'=2,'zlo'=2,'x'=4] {'yhi','zhi'}, dimensions={0} | all-to-all | bytes 1179648 | tf_op jit(solution)/shard_map/all_to_all | solution.py:209
  140.4 0.3 shard_map.130
  140.8 0.0 copy-start.4
  140.8 0.7 copy-done.4
  141.5 7.6 %all-to-all-start.4 = ((bf16[16,24,512]{2,1,0:T(8,128)(2,1)}), bf16[16,24,512]{2,1,0:T(8,128)(2,1)S(1)}, u32[]{:S(2)}, u32[]{:S(2)}) async-start(bf16[16,24,512]{2,1,0:T(8,128)(2,1)} %copy-done.4), calls=%async_computation.4 | async-start | bytes 786432 | tf_op jit(solution)/shard_map/all_to_all | solution.py:209
  149.1 2.3 %shard_map.131 = (bf16[2,64,768]{2,1,0:T(8,128)(2,1)}, bf16[2,64,768]{2,1,0:T(8,128)(2,1)}, bf16[2,64,768]{2,1,0:T(8,128)(2,1)}, bf16[2,64,768]{2,1,0:T(8,128)(2,1)}) custom-call(bf16[512,768]{1,0:T(8,128)(2,1)} %bitcast.15), custom_call_target="tpu_custom_call" | custom-call | flops 10000000 | bytes 1572864 | tf_op jit(solution)/shard_map/pallas_call | solution.py:38
  151.4 11.0 %all-to-all-done.4.rows = bf16[16,24,512]{2,1,0:T(8,128)(2,1)S(1)} async-done(((bf16[16,24,512]{2,1,0:T(8,128)(2,1)}), bf16[16,24,512]{2,1,0:T(8,128)(2,1)S(1)}, u32[]{:S(2)}, u32[]{:S(2)}) %all-to-all-start.4) | async-done | bytes 393248 | tf_op jit(solution)/shard_map/all_to_all | solution.py:209
  162.4 0.2 shard_map.132
  162.6 12.2 %all_to_all.51.by_query = bf16[8,192,128]{2,1,0:T(8,128)(2,1)S(1)} all-to-all(bf16[8,192,128]{2,1,0:T(8,128)(2,1)S(1)} %get-tuple-element.33), channel_id=1, replica_groups=mesh['yhi'=4,'ylo'=2,'zhi'=4,'core'=2,'zlo'=2,'x'=4] {'zlo','x'}, dimensions={0} | all-to-all | bytes 786432 | tf_op jit(solution)/shard_map/all_to_all | solution.py:209
  174.7 1.9 copy-done.3
  176.6 1.1 shard_map.133
  177.8 21.4 %all_to_all.52.heads = bf16[4,4,3,64,128]{4,3,2,1,0:T(8,128)(2,1)} all-to-all(bf16[4,4,3,64,128]{4,3,2,1,0:T(8,128)(2,1)S(1)} %shard_map.133), channel_id=1, replica_groups=mesh['yhi'=4,'ylo'=2,'zhi'=4,'core'=2,'zlo'=2,'x'=4] {'ylo','core'}, dimensions={0} | all-to-all | bytes 1572864 | tf_op jit(solution)/shard_map/all_to_all | solution.py:209
  199.2 2.3 %shard_map.134 = (bf16[2,64,768]{2,1,0:T(8,128)(2,1)}, bf16[2,64,768]{2,1,0:T(8,128)(2,1)}, bf16[2,64,768]{2,1,0:T(8,128)(2,1)}, bf16[2,64,768]{2,1,0:T(8,128)(2,1)}) custom-call(bf16[4,4,3,64,128]{4,3,2,1,0:T(8,128)(2,1)} %all_to_all.52.heads, bf16[2,64,768]{2,1,0:T(8,128)(2,1)} %get-tuple-element.35.col_out), custom_call_target="tpu_custom_call" | custom-call | flops 10000000 | bytes 1769472 | tf_op jit(solution)/shard_map/pallas_call | solution.py:38
  (11 shorter events, 0.0 us)
Async XLA Ops:
  7.2 105.1 %all-gather.5.cloned.1.call-start = ((), (), s32[]{:S(2)}) async-start(), calls=%async_computation.7 | async-start | bytes 3932160 | tf_op jit(solution)/shard_map/all_gather | solution.py:227
  40.2 1.4 copy-start.5
  40.2 1.4 copy-start.6
  40.2 1.4 copy-start.7
  40.2 1.6 copy-start.8
  43.2 34.9 %all-to-all-start.1 = ((bf16[64,8,768]{2,1,0:T(8,128)(2,1)}), bf16[64,8,768]{2,1,0:T(8,128)(2,1)S(1)}, u32[]{:S(2)}, u32[]{:S(2)}) async-start(bf16[64,8,768]{2,1,0:T(8,128)(2,1)} %bitcast.2), calls=%async_computation.1 | async-start | bytes 1572864 | tf_op jit(solution)/shard_map/all_to_all | solution.py:209
  54.1 97.3 %all-gather.7.cloned.1.call-start = ((), (), s32[]{:S(2)}) async-start(), calls=%async_computation.8 | async-start | bytes 3932160 | tf_op jit(solution)/shard_map/all_gather | solution.py:228
  81.2 31.1 %copy-start.2 = (bf16[4,2,2,3,64,128]{5,4,3,2,1,0:T(8,128)(2,1)S(1)}, bf16[4,2,2,3,64,128]{5,4,3,2,1,0:T(8,128)(2,1)}, u32[]{:S(2)}) copy-start(bf16[4,2,2,3,64,128]{5,4,3,2,1,0:T(8,128)(2,1)} %get-tuple-element.27.mine) | copy-start | bytes 2359300
  112.2 1.9 copy-start
  140.4 34.3 %copy-start.1 = (bf16[16,2,2,3,64,128]{5,4,3,2,1,0:T(8,128)(2,1)S(1)}, bf16[16,2,2,3,64,128]{5,4,3,2,1,0:T(8,128)(2,1)}, u32[]{:S(2)}) copy-start(bf16[16,2,2,3,64,128]{5,4,3,2,1,0:T(8,128)(2,1)} %all-gather.5.cloned.1.call-done) | copy-start | bytes 9437188
  140.8 0.8 copy-start.4
  141.5 20.9 %all-to-all-start.4 = ((bf16[16,24,512]{2,1,0:T(8,128)(2,1)}), bf16[16,24,512]{2,1,0:T(8,128)(2,1)S(1)}, u32[]{:S(2)}, u32[]{:S(2)}) async-start(bf16[16,24,512]{2,1,0:T(8,128)(2,1)} %copy-done.4), calls=%async_computation.4 | async-start | bytes 786432 | tf_op jit(solution)/shard_map/all_to_all | solution.py:209
  174.7 1.9 copy-start.3
Sparse Core Ops, SparseCore 0:
  41.7 43.6 all-gather.4
  87.4 45.1 all-gather.6

commit v4 on v3

--- a/solution.py
+++ b/solution.py
@@ -26,20 +26,24 @@
 QR = HL * CB // NRED
 ROW_SCALE = 1.0 / math.sqrt(DH) / math.sqrt(ROWS)
 COL_SCALE = 1.0 / math.sqrt(DH)
+HALVES = (slice(0, COLS // 2), slice(COLS // 2, COLS))
 bf = jnp.bfloat16
 f32 = jnp.float32
 
 
-def call(body, out_shape, *args, scratch=(), inside=True, flops=10**7):
+def call(body, out_shape, *args, scratch=(), inside=True, out_inside=None, flops=10**7):
     many = isinstance(out_shape, (list, tuple))
     outs = out_shape if many else [out_shape]
     nbytes = sum(math.prod(a.shape) * a.dtype.itemsize for a in list(args) + list(outs))
-    spec = pl.BlockSpec(memory_space=pltpu.VMEM) if inside else pl.BlockSpec()
+    spec, out_spec = (
+        pl.BlockSpec(memory_space=pltpu.VMEM) if place else pl.BlockSpec()
+        for place in (inside, inside if out_inside is None else out_inside)
+    )
     return pl.pallas_call(
         body,
         out_shape=out_shape,
         in_specs=[spec] * len(args),
-        out_specs=[spec] * len(outs) if many else spec,
+        out_specs=[out_spec] * len(outs) if many else out_spec,
         scratch_shapes=list(scratch),
         compiler_params=pltpu.CompilerParams(vmem_limit_bytes=(24 if inside else 56) * 2**20),
         cost_estimate=pl.CostEstimate(flops=flops, bytes_accessed=nbytes, transcendentals=0),
@@ -90,15 +94,20 @@
     rest = logits - high
     for m in range(NRED):
         at = slice(m * QR, (m + 1) * QR)
-        out[m] = jnp.concatenate([high[at], rest[at], dprobs[at]], axis=0).astype(bf)
+        out[m] = jnp.concatenate(
+            [a[at, half] for a in (high, rest, dprobs) for half in HALVES], axis=0
+        ).astype(bf)
 
 
 def softmax_kernel(parts, out):
     total = parts[0].astype(f32)
     for m in range(1, NRED):
         total = total + parts[m].astype(f32)
-    logits = (total[:QR] + total[QR : 2 * QR]) * ROW_SCALE
-    dprobs = total[2 * QR :]
+    high, rest, dprobs = (
+        jnp.concatenate([total[n * QR : (n + 1) * QR], total[(n + 1) * QR : (n + 2) * QR]], axis=1)
+        for n in (0, 2, 4)
+    )
+    logits = (high + rest) * ROW_SCALE
     e = jnp.exp(logits - jnp.max(logits, axis=-1, keepdims=True))
     probs = e / jnp.sum(e, axis=-1, keepdims=True)
     dl = probs * (dprobs - jnp.sum(probs * dprobs, axis=-1, keepdims=True)) * ROW_SCALE
@@ -223,25 +232,23 @@
         inside=False,
     )
     mine = swap(by_head.reshape((NHG * NZ,) + by_head.shape[2:]), HGZ).reshape(by_head.shape)
+    cols = call(by_column_kernel, flat, col_q, col_k, col_v, cotangent, scratch=[room])
+    cols, mine = lax.optimization_barrier((cols, mine))
     keys_values, mine = mine[:, :, :2], mine[:, :, 2:]
     keys_values = lax.all_gather(keys_values, "x", axis=0)
     queries_grads = lax.all_gather(mine, "x", axis=0)
 
-    cols = call(
-        by_column_kernel, flat, col_q, col_k, col_v, cotangent, scratch=[room]
-    )
-    cols, mine = lax.optimization_barrier((cols, mine))
     cols = swap(cols, DEP)
     cols = call(column_kernel, flat, cols, scratch=[room], flops=10**9)
     cols = swap(cols, DEP)
-    cols, mine = lax.optimization_barrier((cols, mine))
 
     parts = call(
         logits_kernel,
-        sds((NRED, 3 * QR, COLS), bf),
+        sds((NRED, 6 * QR, COLS // 2), bf),
         mine,
         keys_values,
     )
+    cols, parts = lax.optimization_barrier((cols, parts))
     parts = swap(parts, RED)
     rows = call(softmax_kernel, sds((NRED, 2 * QR, COLS), bf), parts)
     rows = swap(rows, RED)
@@ -270,7 +277,7 @@
     )
     back = swap(back, HG)
     update, grad_rq, grad_rk, grad_rv = call(
-        finish_kernel, [dev] * 4, back, col_out, inside=False
+        finish_kernel, [dev] * 4, back, col_out, out_inside=False
     )
     return update, grad_rq, grad_rk, grad_rv, grad_cq, grad_ck, grad_cv
 

time: 209 us -> 203 us (0.971)
  blocking collectives: 120 us -> 57.7 us
  waiting for transfers between devices: 34.9 us -> 74 us
  starting transfers between devices: 18.5 us -> 35.7 us
    all_to_all x5 -> x3, blocking collectives: 120 us -> 57.7 us  [swap(): return lax.all_to_all(array, axes, 0, 0, tiled=True)]
    all_to_all x2 -> x4, waiting for transfers between devices: 34.2 us -> 73.2 us  [swap(): return lax.all_to_all(array, axes, 0, 0, tiled=True)]
    all_to_all x2 -> x4, starting transfers between devices: 18.5 us -> 35.6 us  [swap(): return lax.all_to_all(array, axes, 0, 0, tiled=True)]
    unnamed x18 -> x22, local copies, waits for them, and re-layouts: 4.78 us -> 5.47 us
  transfers between devices with their start and end apart: 4 -> 6, of which waited for: 2 -> 4; matrix products, arithmetic and copies ran while one was open for 0% -> 0% of each run, Pallas kernels for 4% -> 5%
where the time goes in v4:
time: 203 us
  waiting for transfers between devices  74 us (36%)
  blocking collectives  57.7 us (28%)
  starting transfers between devices  35.7 us (18%)
  Pallas kernels  14.3 us (7%)
  between operations  14.2 us (7%)
  local copies, waits for them, and re-layouts  6.76 us (3%)
    all_to_all x4, waiting for transfers between devices, swap(): return lax.all_to_all(array, axes, 0, 0, tiled=True)  73.2 us
    all_to_all x3, blocking collectives, swap(): return lax.all_to_all(array, axes, 0, 0, tiled=True)  57.7 us
    all_to_all x4, starting transfers between devices, swap(): return lax.all_to_all(array, axes, 0, 0, tiled=True)  35.6 us
    pallas_call x9, Pallas kernels, call(): pl.pallas_call(body, out_shape=out_shape, in_specs=[spec] * len(args), ou...  14.3 us
    unnamed x22, local copies, waits for them, and re-layouts  5.47 us
  transfers between devices with their start and end apart: 6, of which 4 were waited for; matrix products, arithmetic and copies ran while one was open for 0% of the time, Pallas kernels for 5%

profile of v4, /device:TPU:1, one launch (start us, length us, event | category | flops | bytes accessed | tf_op | source)
XLA Modules:
  0.0 202.6 jit_solution(2329065445080887858)
XLA Ops:
  7.2 2.7 %shard_map.127 = bf16[4,2,4,3,64,128]{5,4,3,2,1,0:T(8,128)(2,1)} custom-call(bf16[2,64,768]{2,1,0:T(8,128)(2,1)} %refs_0_.1, bf16[2,64,768]{2,1,0:T(8,128)(2,1)} %refs_1_.1, bf16[2,64,768]{2,1,0:T(8,128)(2,1)} %refs_2_.1, bf16[2,64,768]{2,1,0:T(8,128)(2,1)} %refs_3_.1), custom_call_target="tpu_custom_call" | custom-call | flops 10000000 | bytes 2359296 | tf_op jit(solution)/shard_map/pallas_call | solution.py:42
  9.8 10.5 %all-to-all-start = ((bf16[8,4,3,64,128]{4,3,2,1,0:T(8,128)(2,1)}), bf16[8,4,3,64,128]{4,3,2,1,0:T(8,128)(2,1)S(1)}, u32[]{:S(2)}, u32[]{:S(2)}) async-start(bf16[8,4,3,64,128]{4,3,2,1,0:T(8,128)(2,1)} %bitcast.13), calls=%async_computation | async-start | bytes 3145728 | tf_op jit(solution)/shard_map/all_to_all | solution.py:218
  20.4 0.0 all-gather.5.cloned.1.call-start
  20.4 1.4 shard_map.126
  21.8 18.3 %all-to-all-done = bf16[8,4,3,64,128]{4,3,2,1,0:T(8,128)(2,1)S(1)} async-done(((bf16[8,4,3,64,128]{4,3,2,1,0:T(8,128)(2,1)}), bf16[8,4,3,64,128]{4,3,2,1,0:T(8,128)(2,1)S(1)}, u32[]{:S(2)}, u32[]{:S(2)}) %all-to-all-start) | async-done | bytes 1572896 | tf_op jit(solution)/shard_map/all_to_all | solution.py:218
  40.0 1.3 fusion
  41.3 0.0 all-gather.5.cloned.1.call-update
  41.4 11.3 %all-to-all-start.1 = ((bf16[64,8,768]{2,1,0:T(8,128)(2,1)}), bf16[64,8,768]{2,1,0:T(8,128)(2,1)S(1)}, u32[]{:S(2)}, u32[]{:S(2)}) async-start(bf16[64,8,768]{2,1,0:T(8,128)(2,1)} %bitcast.2), calls=%async_computation.1 | async-start | bytes 1572864 | tf_op jit(solution)/shard_map/all_to_all | solution.py:218
  52.6 0.0 all-gather.7.cloned.1.call-start
  52.7 0.7 all-gather.7.cloned.1.call-update
  53.4 23.2 %all-to-all-done.1 = bf16[64,8,768]{2,1,0:T(8,128)(2,1)S(1)} async-done(((bf16[64,8,768]{2,1,0:T(8,128)(2,1)}), bf16[64,8,768]{2,1,0:T(8,128)(2,1)S(1)}, u32[]{:S(2)}, u32[]{:S(2)}) %all-to-all-start.1) | async-done | bytes 786464 | tf_op jit(solution)/shard_map/all_to_all | solution.py:218
  76.6 4.1 %shard_map.128 = bf16[512,768]{1,0:T(8,128)(2,1)} custom-call(bf16[512,768]{1,0:T(8,128)(2,1)S(1)} %bitcast.11), custom_call_target="tpu_custom_call" | custom-call | flops 1000000000 | bytes 1572864 | tf_op jit(solution)/shard_map/pallas_call | solution.py:42
  80.7 7.2 %all-to-all-start.2 = ((bf16[64,8,768]{2,1,0:T(8,128)(2,1)}), bf16[64,8,768]{2,1,0:T(8,128)(2,1)S(1)}, u32[]{:S(2)}, u32[]{:S(2)}) async-start(bf16[64,8,768]{2,1,0:T(8,128)(2,1)} %bitcast.4), calls=%async_computation.2 | async-start | bytes 1572864 | tf_op jit(solution)/shard_map/all_to_all | solution.py:218
  87.9 0.0 all-gather.5.cloned.1.call-done
  87.9 1.9 copy-done
  89.8 1.1 shard_map.129
  91.0 20.9 %all-to-all-done.2 = bf16[64,8,768]{2,1,0:T(8,128)(2,1)S(1)} async-done(((bf16[64,8,768]{2,1,0:T(8,128)(2,1)}), bf16[64,8,768]{2,1,0:T(8,128)(2,1)S(1)}, u32[]{:S(2)}, u32[]{:S(2)}) %all-to-all-start.2) | async-done | bytes 786464 | tf_op jit(solution)/shard_map/all_to_all | solution.py:218
  111.8 0.9 copy-done.10
  112.7 24.7 %all_to_all.48.parts = bf16[16,72,256]{2,1,0:T(8,128)(2,1)S(1)} all-to-all(bf16[16,72,256]{2,1,0:T(8,128)(2,1)S(1)} %shard_map.129), channel_id=1, replica_groups=mesh['yhi'=4,'ylo'=2,'zhi'=4,'core'=2,'zlo'=2,'x'=4] {'yhi','zhi'}, dimensions={0} | all-to-all | bytes 1179648 | tf_op jit(solution)/shard_map/all_to_all | solution.py:218
  137.5 0.3 shard_map.130
  137.8 0.0 copy-start.4
  137.8 0.8 copy-done.4
  138.6 6.6 %all-to-all-start.4 = ((bf16[16,24,512]{2,1,0:T(8,128)(2,1)}), bf16[16,24,512]{2,1,0:T(8,128)(2,1)S(1)}, u32[]{:S(2)}, u32[]{:S(2)}) async-start(bf16[16,24,512]{2,1,0:T(8,128)(2,1)} %copy-done.4), calls=%async_computation.4 | async-start | bytes 786432 | tf_op jit(solution)/shard_map/all_to_all | solution.py:218
  145.2 2.3 %shard_map.131 = (bf16[2,64,768]{2,1,0:T(8,128)(2,1)}, bf16[2,64,768]{2,1,0:T(8,128)(2,1)}, bf16[2,64,768]{2,1,0:T(8,128)(2,1)}, bf16[2,64,768]{2,1,0:T(8,128)(2,1)}) custom-call(bf16[512,768]{1,0:T(8,128)(2,1)} %bitcast.14), custom_call_target="tpu_custom_call" | custom-call | flops 10000000 | bytes 1572864 | tf_op jit(solution)/shard_map/pallas_call | solution.py:42
  147.6 10.9 %all-to-all-done.4.rows = bf16[16,24,512]{2,1,0:T(8,128)(2,1)S(1)} async-done(((bf16[16,24,512]{2,1,0:T(8,128)(2,1)}), bf16[16,24,512]{2,1,0:T(8,128)(2,1)S(1)}, u32[]{:S(2)}, u32[]{:S(2)}) %all-to-all-start.4) | async-done | bytes 393248 | tf_op jit(solution)/shard_map/all_to_all | solution.py:218
  158.5 0.2 shard_map.132
  158.6 11.5 %all_to_all.49.by_query = bf16[8,192,128]{2,1,0:T(8,128)(2,1)S(1)} all-to-all(bf16[8,192,128]{2,1,0:T(8,128)(2,1)S(1)} %get-tuple-element.33), channel_id=1, replica_groups=mesh['yhi'=4,'ylo'=2,'zhi'=4,'core'=2,'zlo'=2,'x'=4] {'zlo','x'}, dimensions={0} | all-to-all | bytes 786432 | tf_op jit(solution)/shard_map/all_to_all | solution.py:218
  170.2 1.9 copy-done.3
  172.1 1.1 shard_map.133
  173.2 0.0 copy-start.9
  173.2 21.4 %all_to_all.50.heads = bf16[4,4,3,64,128]{4,3,2,1,0:T(8,128)(2,1)S(1)} all-to-all(bf16[4,4,3,64,128]{4,3,2,1,0:T(8,128)(2,1)S(1)} %shard_map.133), channel_id=1, replica_groups=mesh['yhi'=4,'ylo'=2,'zhi'=4,'core'=2,'zlo'=2,'x'=4] {'ylo','core'}, dimensions={0} | all-to-all | bytes 1572864 | tf_op jit(solution)/shard_map/all_to_all | solution.py:218
  194.6 1.1 shard_map.134
  (17 shorter events, 0.0 us)
Async XLA Ops:
  9.8 10.5 %copy-start.5 = (bf16[2,64,768]{2,1,0:T(8,128)(2,1)S(1)}, bf16[2,64,768]{2,1,0:T(8,128)(2,1)}, u32[]{:S(2)}) copy-start(bf16[2,64,768]{2,1,0:T(8,128)(2,1)} %refs_3_.1) | copy-start | bytes 589828
  9.8 10.5 %copy-start.6 = (bf16[2,64,768]{2,1,0:T(8,128)(2,1)S(1)}, bf16[2,64,768]{2,1,0:T(8,128)(2,1)}, u32[]{:S(2)}) copy-start(bf16[2,64,768]{2,1,0:T(8,128)(2,1)} %query.1) | copy-start | bytes 589828
  9.8 10.5 %copy-start.7 = (bf16[2,64,768]{2,1,0:T(8,128)(2,1)S(1)}, bf16[2,64,768]{2,1,0:T(8,128)(2,1)}, u32[]{:S(2)}) copy-start(bf16[2,64,768]{2,1,0:T(8,128)(2,1)} %keys.1) | copy-start | bytes 589828
  9.8 10.5 %copy-start.8 = (bf16[2,64,768]{2,1,0:T(8,128)(2,1)S(1)}, bf16[2,64,768]{2,1,0:T(8,128)(2,1)}, u32[]{:S(2)}) copy-start(bf16[2,64,768]{2,1,0:T(8,128)(2,1)} %values.1) | copy-start | bytes 589828
  9.8 30.2 %all-to-all-start = ((bf16[8,4,3,64,128]{4,3,2,1,0:T(8,128)(2,1)}), bf16[8,4,3,64,128]{4,3,2,1,0:T(8,128)(2,1)S(1)}, u32[]{:S(2)}, u32[]{:S(2)}) async-start(bf16[8,4,3,64,128]{4,3,2,1,0:T(8,128)(2,1)} %bitcast.13), calls=%async_computation | async-start | bytes 3145728 | tf_op jit(solution)/shard_map/all_to_all | solution.py:218
  20.4 67.5 %all-gather.5.cloned.1.call-start = ((), (), s32[]{:S(2)}) async-start(), calls=%async_computation.7 | async-start | bytes 3932160 | tf_op jit(solution)/shard_map/all_gather | solution.py:238
  41.4 35.2 %all-to-all-start.1 = ((bf16[64,8,768]{2,1,0:T(8,128)(2,1)}), bf16[64,8,768]{2,1,0:T(8,128)(2,1)S(1)}, u32[]{:S(2)}, u32[]{:S(2)}) async-start(bf16[64,8,768]{2,1,0:T(8,128)(2,1)} %bitcast.2), calls=%async_computation.1 | async-start | bytes 1572864 | tf_op jit(solution)/shard_map/all_to_all | solution.py:218
  52.6 94.9 %all-gather.7.cloned.1.call-start = ((), (), s32[]{:S(2)}) async-start(), calls=%async_computation.8 | async-start | bytes 3932160 | tf_op jit(solution)/shard_map/all_gather | solution.py:239
  80.7 7.2 %copy-start.2 = (bf16[4,2,2,3,64,128]{5,4,3,2,1,0:T(8,128)(2,1)S(1)}, bf16[4,2,2,3,64,128]{5,4,3,2,1,0:T(8,128)(2,1)}, u32[]{:S(2)}) copy-start(bf16[4,2,2,3,64,128]{5,4,3,2,1,0:T(8,128)(2,1)} %get-tuple-element.44.mine) | copy-start | bytes 2359300
  80.7 31.1 %all-to-all-start.2 = ((bf16[64,8,768]{2,1,0:T(8,128)(2,1)}), bf16[64,8,768]{2,1,0:T(8,128)(2,1)S(1)}, u32[]{:S(2)}, u32[]{:S(2)}) async-start(bf16[64,8,768]{2,1,0:T(8,128)(2,1)} %bitcast.4), calls=%async_computation.2 | async-start | bytes 1572864 | tf_op jit(solution)/shard_map/all_to_all | solution.py:218
  87.9 1.9 copy-start
  111.8 0.9 copy-start.10
  137.5 32.7 %copy-start.1 = (bf16[16,2,2,3,64,128]{5,4,3,2,1,0:T(8,128)(2,1)S(1)}, bf16[16,2,2,3,64,128]{5,4,3,2,1,0:T(8,128)(2,1)}, u32[]{:S(2)}) copy-start(bf16[16,2,2,3,64,128]{5,4,3,2,1,0:T(8,128)(2,1)} %all-gather.5.cloned.1.call-done) | copy-start | bytes 9437188
  137.8 0.8 copy-start.4
  138.6 19.9 %all-to-all-start.4 = ((bf16[16,24,512]{2,1,0:T(8,128)(2,1)}), bf16[16,24,512]{2,1,0:T(8,128)(2,1)S(1)}, u32[]{:S(2)}, u32[]{:S(2)}) async-start(bf16[16,24,512]{2,1,0:T(8,128)(2,1)} %copy-done.4), calls=%async_computation.4 | async-start | bytes 786432 | tf_op jit(solution)/shard_map/all_to_all | solution.py:218
  170.2 1.9 copy-start.3
  173.2 21.4 %copy-start.9 = (bf16[2,64,768]{2,1,0:T(8,128)(2,1)S(1)}, bf16[2,64,768]{2,1,0:T(8,128)(2,1)}, u32[]{:S(2)}) copy-start(bf16[2,64,768]{2,1,0:T(8,128)(2,1)} %get-tuple-element.35.col_out) | copy-start | bytes 589828
Sparse Core Ops, SparseCore 0:
  41.5 43.9 all-gather.4
  87.6 45.1 all-gather.6

commit v5 on v4

--- a/solution.py
+++ b/solution.py
@@ -11,17 +11,20 @@
 DH = 64
 ROWS = 128
 COLS = 512
-HG = ("ylo", "core")
-HGZ = ("ylo", "core", "zlo")
+NEAR = ("ylo", "zlo", "core")
 RED = ("yhi", "zhi")
 DEP = ("yhi", "ylo", "zhi", "core")
 RES = ("zlo", "x")
+BLOCKS = ("core", "x")
 NHG = 4
+SEQS = ((0, 0), (0, 1), (1, 0), (1, 1))
 HL = 3
 NRED = 16
 NRES = 8
 NX = 4
 NZ = 2
+NC = 2
+HC = 32
 CB = 64
 QR = HL * CB // NRED
 ROW_SCALE = 1.0 / math.sqrt(DH) / math.sqrt(ROWS)
@@ -35,17 +38,19 @@
     many = isinstance(out_shape, (list, tuple))
     outs = out_shape if many else [out_shape]
     nbytes = sum(math.prod(a.shape) * a.dtype.itemsize for a in list(args) + list(outs))
-    spec, out_spec = (
-        pl.BlockSpec(memory_space=pltpu.VMEM) if place else pl.BlockSpec()
-        for place in (inside, inside if out_inside is None else out_inside)
-    )
+    specs = {
+        True: pl.BlockSpec(memory_space=pltpu.VMEM),
+        False: pl.BlockSpec(),
+        "far": pl.BlockSpec(memory_space=pl.ANY),
+    }
+    spec, out_spec = specs[inside], specs[inside if out_inside is None else out_inside]
     return pl.pallas_call(
         body,
         out_shape=out_shape,
         in_specs=[spec] * len(args),
         out_specs=[out_spec] * len(outs) if many else out_spec,
         scratch_shapes=list(scratch),
-        compiler_params=pltpu.CompilerParams(vmem_limit_bytes=(24 if inside else 56) * 2**20),
+        compiler_params=pltpu.CompilerParams(vmem_limit_bytes=(24 if inside is True else 56) * 2**20),
         cost_estimate=pl.CostEstimate(flops=flops, bytes_accessed=nbytes, transcendentals=0),
     )(*args)
 
@@ -59,34 +64,48 @@
 
 
 def to_heads_kernel(*refs):
-    out = refs[-1]
-    for n, ref in enumerate(refs[:-1]):
+    arrays, (out, got, made, in_sems, out_sems) = refs[:4], refs[4:]
+    reads = [
+        pltpu.make_async_copy(ref, got.at[n], in_sems.at[n]) for n, ref in enumerate(arrays)
+    ]
+    for copy in reads:
+        copy.start()
+    writes = []
+    for n, read in enumerate(reads):
+        read.wait()
         for h in range(H):
-            a = ref[0, :, h * DH : (h + 1) * DH]
-            b = ref[1, :, h * DH : (h + 1) * DH]
+            a = got[n, 0, :, h * DH : (h + 1) * DH]
+            b = got[n, 1, :, h * DH : (h + 1) * DH]
             both = jnp.concatenate([a, b], axis=1)
-            for z in range(NZ):
-                out[h // HL, z, n, h % HL] = both
+            for c in range(NC):
+                made[n, h // HL * NC + c, h % HL] = both[c * HC : (c + 1) * HC]
+        writes.append(pltpu.make_async_copy(made.at[n], out.at[:, n], out_sems.at[n]))
+        writes[-1].start()
+    for copy in writes:
+        copy.wait()
+
+
+def block(ref, at, n, h):
+    return jnp.concatenate(
+        [
+            jnp.concatenate([ref[(*at, (y * NZ + z) * NC + c, n, h)] for y, c in SEQS], axis=1)
+            for z in range(NZ)
+        ],
+        axis=0,
+    )
 
 
 def gathered(ref, n, h):
     return jnp.concatenate(
-        [
-            jnp.concatenate([ref[x, s, z, n, h] for s in range(NHG)], axis=1)
-            for z in range(NZ)
-            for x in range(NX)
-        ],
-        axis=0,
+        [block(ref, (x, c), n, h) for c in range(NC) for x in range(NX)], axis=0
     )
 
 
 def logits_kernel(mine, keys_values, out):
-    own = lax.axis_index("zlo")
     logits, dprobs = [], []
     for h in range(HL):
         for res, n, which in ((logits, 0, 0), (dprobs, 1, 1)):
-            lhs = jnp.concatenate([mine[s, own, n, h] for s in range(NHG)], axis=1)
-            res.append(dot(lhs, gathered(keys_values, which, h), 1, 1))
+            res.append(dot(block(mine, (), n, h), gathered(keys_values, which, h), 1, 1))
     logits = jnp.concatenate(logits, axis=0)
     dprobs = jnp.concatenate(dprobs, axis=0)
     dprobs = dprobs - jnp.mean(dprobs, axis=-1, keepdims=True)
@@ -131,8 +150,11 @@
 def row_grads_kernel(probs, dlogits, by_query, keys_values, queries_grads, out):
 
     def put(n, h, res):
-        for s in range(NHG):
-            out[s, n, h] = res[:, s * 2 * DH : (s + 1) * 2 * DH].astype(bf)
+        for z in range(NZ):
+            for s, (y, c) in enumerate(SEQS):
+                out[(y * NZ + z) * NC + c, n, h] = res[
+                    z * HC : (z + 1) * HC, s * 2 * DH : (s + 1) * 2 * DH
+                ].astype(bf)
 
     for h in range(HL):
         at = slice(h * CB, (h + 1) * CB)
@@ -152,7 +174,7 @@
         out[:, at] = rows[pair].astype(bf)
 
 
-def column_kernel(got, out, rows):
+def column_kernel(got, out, rows, made, sems):
     low = lax.broadcasted_iota(jnp.int32, (ROWS, 2 * DH), 1) < DH
     zero = jnp.zeros((ROWS, 2 * DH), bf)
 
@@ -162,6 +184,7 @@
     def beside(x):
         return jnp.concatenate([x[:ROWS], x[ROWS:]], axis=1)
 
+    copies = []
     for pair in range(H // 2):
         at = slice(pair * 2 * DH, (pair + 1) * 2 * DH)
         rows[pair] = got[:, at].astype(f32)
@@ -188,7 +211,11 @@
         for n in range(4):
             for r in range(2):
                 rows[pair, pl.ds(2 * n + r, CB, stride=8), :] = res[n][r * CB : (r + 1) * CB]
-        out[:, at] = rows[pair].astype(bf)
+        made[pair] = rows[pair].astype(bf)
+        copies.append(pltpu.make_async_copy(made.at[pair], out.at[:, at], sems.at[pair]))
+        copies[-1].start()
+    for copy in copies:
+        copy.wait()
 
 
 def column_finish_kernel(columns, col_out, grad_cq, grad_ck, grad_cv, rows):
@@ -204,7 +231,10 @@
     for pair in range(H // 2):
         at = slice(pair * 2 * DH, (pair + 1) * 2 * DH)
         for n, ref in enumerate((update, grad_rq, grad_rk, grad_rv)):
-            a, b = (heads[h // HL, n, h % HL] for h in (2 * pair, 2 * pair + 1))
+            a, b = (
+                jnp.concatenate([heads[h // HL * NC + c, n, h % HL] for c in range(NC)], axis=0)
+                for h in (2 * pair, 2 * pair + 1)
+            )
             for r in range(2):
                 got = jnp.concatenate(
                     [a[:, r * DH : (r + 1) * DH], b[:, r * DH : (r + 1) * DH]], axis=1
@@ -224,22 +254,47 @@
     room = pltpu.VMEM((H // 2, CB * 8, 2 * DH), f32)
     by_head = call(
         to_heads_kernel,
-        sds((NHG, NZ, 4, HL, CB, 2 * DH), bf),
+        sds((NHG * NC, 4, HL, HC, 2 * DH), bf),
         row_k,
         row_v,
         row_q,
         cotangent,
-        inside=False,
-    )
-    mine = swap(by_head.reshape((NHG * NZ,) + by_head.shape[2:]), HGZ).reshape(by_head.shape)
+        scratch=[
+            pltpu.VMEM((4, 2, CB, H * DH), bf),
+            pltpu.VMEM((4, NHG * NC, HL, HC, 2 * DH), bf),
+            pltpu.SemaphoreType.DMA((4,)),
+            pltpu.SemaphoreType.DMA((4,)),
+        ],
+        inside="far",
+    )
+    mine = swap(by_head, NEAR)
     cols = call(by_column_kernel, flat, col_q, col_k, col_v, cotangent, scratch=[room])
     cols, mine = lax.optimization_barrier((cols, mine))
-    keys_values, mine = mine[:, :, :2], mine[:, :, 2:]
-    keys_values = lax.all_gather(keys_values, "x", axis=0)
-    queries_grads = lax.all_gather(mine, "x", axis=0)
+    first = lax.axis_index("core") == 0
+    other = lax.ppermute(mine, "core", [(0, 1), (1, 0)])
+
+    def spread(n):
+        own, far = mine[:, n : n + 2], other[:, n : n + 2]
+        both = jnp.stack([jnp.where(first, own, far), jnp.where(first, far, own)])
+        return lax.all_gather(both, "x", axis=0)
+
+    keys_values = spread(0)
+    queries_grads = spread(2)
+    mine = mine[:, 2:]
 
     cols = swap(cols, DEP)
-    cols = call(column_kernel, flat, cols, scratch=[room], flops=10**9)
+    cols = call(
+        column_kernel,
+        flat,
+        cols,
+        scratch=[
+            room,
+            pltpu.VMEM((H // 2, CB * 8, 2 * DH), bf),
+            pltpu.SemaphoreType.DMA((H // 2,)),
+        ],
+        out_inside="far",
+        flops=10**9,
+    )
     cols = swap(cols, DEP)
 
     parts = call(
@@ -265,17 +320,17 @@
         ],
         rows,
     )
-    by_query = swap(by_key, RES)
+    by_query = swap(by_key, BLOCKS)
     back = call(
         row_grads_kernel,
-        sds((NHG, 4, HL, CB, 2 * DH), bf),
+        sds((NHG * NC, 4, HL, HC, 2 * DH), bf),
         probs,
         dlogits,
         by_query,
         keys_values,
         queries_grads,
     )
-    back = swap(back, HG)
+    back = swap(back, NEAR)
     update, grad_rq, grad_rk, grad_rv = call(
         finish_kernel, [dev] * 4, back, col_out, out_inside=False
     )

time: 203 us -> 197 us (0.970)
  waiting for transfers between devices: 74 us -> 65.1 us
  starting transfers between devices: 35.7 us -> 38 us
  other arithmetic: 0 us -> 2.06 us
    all_to_all x4, waiting for transfers between devices: 73.2 us -> 63.2 us  [swap(): return lax.all_to_all(array, axes, 0, 0, tiled=True)]
    ppermute x0 -> x1, starting transfers between devices: none -> 2.77 us  [on_device(): other = lax.ppermute(mine, 'core', [(0, 1), (1, 0)])]
    another operation x0 -> x3, other arithmetic: none -> 2.06 us  [spread(): both = jnp.stack([jnp.where(first, own, far), jnp.where(first, far, own)])]
    unnamed x22 -> x20, local copies, waits for them, and re-layouts: 5.47 us -> 5.34 us
  transfers between devices with their start and end apart: 6 -> 7, of which waited for: 4 -> 5; matrix products, arithmetic and copies ran while one was open for 0% -> 0% of each run, Pallas kernels for 5% -> 5%
where the time goes in v5:
time: 197 us
  waiting for transfers between devices  65.1 us (33%)
  blocking collectives  58.2 us (30%)
  starting transfers between devices  38 us (19%)
  between operations  14.2 us (7%)
  Pallas kernels  13.7 us (7%)
  local copies, waits for them, and re-layouts  5.34 us (3%)
  other arithmetic  2.06 us (1%)
    all_to_all x4, waiting for transfers between devices, swap(): return lax.all_to_all(array, axes, 0, 0, tiled=True)  63.2 us
    all_to_all x3, blocking collectives, swap(): return lax.all_to_all(array, axes, 0, 0, tiled=True)  58.2 us
    all_to_all x4, starting transfers between devices, swap(): return lax.all_to_all(array, axes, 0, 0, tiled=True)  35.2 us
    pallas_call x9, Pallas kernels, call(): pl.pallas_call(body, out_shape=out_shape, in_specs=[spec] * len(args), ou...  13.7 us
    unnamed x20, local copies, waits for them, and re-layouts  5.34 us
  transfers between devices with their start and end apart: 7, of which 5 were waited for; matrix products, arithmetic and copies ran while one was open for 0% of the time, Pallas kernels for 5%

profile of v5, /device:TPU:1, one launch (start us, length us, event | category | flops | bytes accessed | tf_op | source)
XLA Modules:
  0.0 196.6 jit_solution(277040414589176569)
XLA Ops:
  7.2 2.2 %shard_map.127 = bf16[8,4,3,32,128]{4,3,2,1,0:T(8,128)(2,1)} custom-call(bf16[2,64,768]{2,1,0:T(8,128)(2,1)} %refs_0_.1, bf16[2,64,768]{2,1,0:T(8,128)(2,1)} %refs_1_.1, bf16[2,64,768]{2,1,0:T(8,128)(2,1)} %refs_2_.1, bf16[2,64,768]{2,1,0:T(8,128)(2,1)} %refs_3_.1), custom_call_target="tpu_custom_call" | custom-call | flops 10000000 | bytes 1572864 | tf_op jit(solution)/shard_map/pallas_call | solution.py:47
  9.4 10.3 %all-to-all-start = ((bf16[8,4,3,32,128]{4,3,2,1,0:T(8,128)(2,1)}), bf16[8,4,3,32,128]{4,3,2,1,0:T(8,128)(2,1)S(1)}, u32[]{:S(2)}, u32[]{:S(2)}) async-start(bf16[8,4,3,32,128]{4,3,2,1,0:T(8,128)(2,1)} %shard_map.127), calls=%async_computation | async-start | bytes 1572864 | tf_op jit(solution)/shard_map/all_to_all | solution.py:248
  19.8 1.4 shard_map.126
  21.2 9.4 %all-to-all-done = bf16[8,4,3,32,128]{4,3,2,1,0:T(8,128)(2,1)S(1)} async-done(((bf16[8,4,3,32,128]{4,3,2,1,0:T(8,128)(2,1)}), bf16[8,4,3,32,128]{4,3,2,1,0:T(8,128)(2,1)S(1)}, u32[]{:S(2)}, u32[]{:S(2)}) %all-to-all-start) | async-done | bytes 786464 | tf_op jit(solution)/shard_map/all_to_all | solution.py:248
  30.6 2.8 %collective-permute-start = (bf16[8,4,3,32,128]{4,3,2,1,0:T(8,128)(2,1)S(1)}, bf16[8,4,3,32,128]{4,3,2,1,0:T(8,128)(2,1)S(1)}, u32[]{:S(2)}, u32[]{:S(2)}) collective-permute-start(bf16[8,4,3,32,128]{4,3,2,1,0:T(8,128)(2,1)S(1)} %all-to-all-done), channel_id=1, source_target_pairs={{0,8},{8,0},{1,9},{9,1},{2,10},{10,2},{3,11},{11,3},{4,12},{12,4},... | collective-permute-start | bytes 2359304 | tf_op jit(solution)/shard_map/ppermute | solution.py:274
  33.4 1.9 collective-permute-done
  35.2 0.1 select_bitcast_fusion.1
  35.4 1.0 pad_maximum_fusion
  36.3 0.0 all-gather.5.cloned.1.call-update
  36.4 11.1 %all-to-all-start.1 = ((bf16[64,8,768]{2,1,0:T(8,128)(2,1)}), bf16[64,8,768]{2,1,0:T(8,128)(2,1)S(1)}, u32[]{:S(2)}, u32[]{:S(2)}) async-start(bf16[64,8,768]{2,1,0:T(8,128)(2,1)} %bitcast), calls=%async_computation.1 | async-start | bytes 1572864 | tf_op jit(solution)/shard_map/all_to_all | solution.py:248
  47.5 0.0 all-gather.7.cloned.1.call-start
  47.6 1.0 pad_maximum_fusion.1
  48.6 22.9 %all-to-all-done.1 = bf16[64,8,768]{2,1,0:T(8,128)(2,1)S(1)} async-done(((bf16[64,8,768]{2,1,0:T(8,128)(2,1)}), bf16[64,8,768]{2,1,0:T(8,128)(2,1)S(1)}, u32[]{:S(2)}, u32[]{:S(2)}) %all-to-all-start.1) | async-done | bytes 786464 | tf_op jit(solution)/shard_map/all_to_all | solution.py:248
  71.5 3.9 %shard_map.128 = bf16[512,768]{1,0:T(8,128)(2,1)} custom-call(bf16[512,768]{1,0:T(8,128)(2,1)S(1)} %bitcast.17), custom_call_target="tpu_custom_call" | custom-call | flops 1000000000 | bytes 1572864 | tf_op jit(solution)/shard_map/pallas_call | solution.py:47
  75.3 7.2 %all-to-all-start.2 = ((bf16[64,8,768]{2,1,0:T(8,128)(2,1)}), bf16[64,8,768]{2,1,0:T(8,128)(2,1)}, u32[]{:S(2)}, u32[]{:S(2)}) async-start(bf16[64,8,768]{2,1,0:T(8,128)(2,1)} %bitcast.2), calls=%async_computation.2 | async-start | bytes 1572864 | tf_op jit(solution)/shard_map/all_to_all | solution.py:248
  82.6 0.0 all-gather.5.cloned.1.call-done
  82.6 1.9 copy-done
  84.5 1.1 shard_map.129
  85.7 0.8 copy-done.3
  86.5 20.0 %all-to-all-done.2 = bf16[64,8,768]{2,1,0:T(8,128)(2,1)} async-done(((bf16[64,8,768]{2,1,0:T(8,128)(2,1)}), bf16[64,8,768]{2,1,0:T(8,128)(2,1)}, u32[]{:S(2)}, u32[]{:S(2)}) %all-to-all-start.2) | async-done | bytes 786464 | tf_op jit(solution)/shard_map/all_to_all | solution.py:248
  106.5 25.0 %all_to_all.48.parts = bf16[16,72,256]{2,1,0:T(8,128)(2,1)S(1)} all-to-all(bf16[16,72,256]{2,1,0:T(8,128)(2,1)} %copy-done.3), channel_id=1, replica_groups=mesh['yhi'=4,'ylo'=2,'zhi'=4,'core'=2,'zlo'=2,'x'=4] {'yhi','zhi'}, dimensions={0} | all-to-all | bytes 1179648 | tf_op jit(solution)/shard_map/all_to_all | solution.py:248
  131.5 0.3 shard_map.130
  131.8 0.7 copy-done.4
  132.5 6.4 %all-to-all-start.4 = ((bf16[16,24,512]{2,1,0:T(8,128)(2,1)}), bf16[16,24,512]{2,1,0:T(8,128)(2,1)S(1)}, u32[]{:S(2)}, u32[]{:S(2)}) async-start(bf16[16,24,512]{2,1,0:T(8,128)(2,1)} %copy-done.4), calls=%async_computation.4 | async-start | bytes 786432 | tf_op jit(solution)/shard_map/all_to_all | solution.py:248
  139.0 2.3 %shard_map.131 = (bf16[2,64,768]{2,1,0:T(8,128)(2,1)}, bf16[2,64,768]{2,1,0:T(8,128)(2,1)}, bf16[2,64,768]{2,1,0:T(8,128)(2,1)}, bf16[2,64,768]{2,1,0:T(8,128)(2,1)}) custom-call(bf16[512,768]{1,0:T(8,128)(2,1)} %bitcast.3.columns), custom_call_target="tpu_custom_call" | custom-call | flops 10000000 | bytes 1572864 | tf_op jit(solution)/shard_map/pallas_call | solution.py:47
  141.3 10.9 %all-to-all-done.4.rows = bf16[16,24,512]{2,1,0:T(8,128)(2,1)S(1)} async-done(((bf16[16,24,512]{2,1,0:T(8,128)(2,1)}), bf16[16,24,512]{2,1,0:T(8,128)(2,1)S(1)}, u32[]{:S(2)}, u32[]{:S(2)}) %all-to-all-start.4) | async-done | bytes 393248 | tf_op jit(solution)/shard_map/all_to_all | solution.py:248
  152.2 0.2 shard_map.132
  152.4 14.6 %all_to_all.49.by_query = bf16[8,192,128]{2,1,0:T(8,128)(2,1)S(1)} all-to-all(bf16[8,192,128]{2,1,0:T(8,128)(2,1)S(1)} %get-tuple-element.33), channel_id=1, replica_groups=mesh['yhi'=4,'ylo'=2,'zhi'=4,'core'=2,'zlo'=2,'x'=4] {'core','x'}, dimensions={0} | all-to-all | bytes 786432 | tf_op jit(solution)/shard_map/all_to_all | solution.py:248
  167.0 1.9 copy-done.2
  168.9 1.1 shard_map.133
  170.0 18.6 %all_to_all.50.heads = bf16[8,4,3,32,128]{4,3,2,1,0:T(8,128)(2,1)S(1)} all-to-all(bf16[8,4,3,32,128]{4,3,2,1,0:T(8,128)(2,1)S(1)} %shard_map.133), channel_id=1, replica_groups=mesh['yhi'=4,'ylo'=2,'zhi'=4,'core'=2,'zlo'=2,'x'=4] {'ylo','zlo','core'}, dimensions={0} | all-to-all | bytes 1572864 | tf_op jit(solution)/shard_map/all_to_all | solution.py:248
  188.7 1.1 shard_map.134
  (19 shorter events, 0.1 us)
Async XLA Ops:
  7.2 12.6 %copy-start.5 = (bf16[2,64,768]{2,1,0:T(8,128)(2,1)S(1)}, bf16[2,64,768]{2,1,0:T(8,128)(2,1)}, u32[]{:S(2)}) copy-start(bf16[2,64,768]{2,1,0:T(8,128)(2,1)} %refs_3_.1) | copy-start | bytes 589828
  7.2 12.6 %copy-start.8 = (bf16[2,64,768]{2,1,0:T(8,128)(2,1)S(1)}, bf16[2,64,768]{2,1,0:T(8,128)(2,1)}, u32[]{:S(2)}) copy-start(bf16[2,64,768]{2,1,0:T(8,128)(2,1)} %values.1) | copy-start | bytes 589828
  7.2 12.6 %copy-start.7 = (bf16[2,64,768]{2,1,0:T(8,128)(2,1)S(1)}, bf16[2,64,768]{2,1,0:T(8,128)(2,1)}, u32[]{:S(2)}) copy-start(bf16[2,64,768]{2,1,0:T(8,128)(2,1)} %keys.1) | copy-start | bytes 589828
  7.2 12.6 %copy-start.6 = (bf16[2,64,768]{2,1,0:T(8,128)(2,1)S(1)}, bf16[2,64,768]{2,1,0:T(8,128)(2,1)}, u32[]{:S(2)}) copy-start(bf16[2,64,768]{2,1,0:T(8,128)(2,1)} %query.1) | copy-start | bytes 589828
  9.4 21.1 %all-to-all-start = ((bf16[8,4,3,32,128]{4,3,2,1,0:T(8,128)(2,1)}), bf16[8,4,3,32,128]{4,3,2,1,0:T(8,128)(2,1)S(1)}, u32[]{:S(2)}, u32[]{:S(2)}) async-start(bf16[8,4,3,32,128]{4,3,2,1,0:T(8,128)(2,1)} %shard_map.127), calls=%async_computation | async-start | bytes 1572864 | tf_op jit(solution)/shard_map/all_to_all | solution.py:248
  19.8 62.8 %all-gather.5.cloned.1.call-start = ((), (), s32[]{:S(2)}) async-start(), calls=%async_computation.7 | async-start | bytes 3932160 | tf_op jit(solution)/shard_map/all_gather | solution.py:279
  30.6 4.7 %collective-permute-start = (bf16[8,4,3,32,128]{4,3,2,1,0:T(8,128)(2,1)S(1)}, bf16[8,4,3,32,128]{4,3,2,1,0:T(8,128)(2,1)S(1)}, u32[]{:S(2)}, u32[]{:S(2)}) collective-permute-start(bf16[8,4,3,32,128]{4,3,2,1,0:T(8,128)(2,1)S(1)} %all-to-all-done), channel_id=1, source_target_pairs={{0,8},{8,0},{1,9},{9,1},{2,10},{10,2},{3,11},{11,3},{4,12},{12,4},... | collective-permute-start | bytes 2359304 | tf_op jit(solution)/shard_map/ppermute | solution.py:274
  36.4 35.1 %all-to-all-start.1 = ((bf16[64,8,768]{2,1,0:T(8,128)(2,1)}), bf16[64,8,768]{2,1,0:T(8,128)(2,1)S(1)}, u32[]{:S(2)}, u32[]{:S(2)}) async-start(bf16[64,8,768]{2,1,0:T(8,128)(2,1)} %bitcast), calls=%async_computation.1 | async-start | bytes 1572864 | tf_op jit(solution)/shard_map/all_to_all | solution.py:248
  47.5 93.8 %all-gather.7.cloned.1.call-start = ((), (), s32[]{:S(2)}) async-start(), calls=%async_computation.8 | async-start | bytes 3932160 | tf_op jit(solution)/shard_map/all_gather | solution.py:279
  75.3 31.1 %all-to-all-start.2 = ((bf16[64,8,768]{2,1,0:T(8,128)(2,1)}), bf16[64,8,768]{2,1,0:T(8,128)(2,1)}, u32[]{:S(2)}, u32[]{:S(2)}) async-start(bf16[64,8,768]{2,1,0:T(8,128)(2,1)} %bitcast.2), calls=%async_computation.2 | async-start | bytes 1572864 | tf_op jit(solution)/shard_map/all_to_all | solution.py:248
  82.6 1.9 copy-start
  85.7 0.8 copy-start.3
  86.5 80.5 %copy-start.1 = (bf16[8,8,2,3,32,128]{5,4,3,2,1,0:T(8,128)(2,1)S(1)}, bf16[8,8,2,3,32,128]{5,4,3,2,1,0:T(8,128)(2,1)}, u32[]{:S(2)}) copy-start(bf16[8,8,2,3,32,128]{5,4,3,2,1,0:T(8,128)(2,1)} %all-gather.5.cloned.1.call-done) | copy-start | bytes 9437188
  131.8 0.7 copy-start.4
  132.5 19.7 %all-to-all-start.4 = ((bf16[16,24,512]{2,1,0:T(8,128)(2,1)}), bf16[16,24,512]{2,1,0:T(8,128)(2,1)S(1)}, u32[]{:S(2)}, u32[]{:S(2)}) async-start(bf16[16,24,512]{2,1,0:T(8,128)(2,1)} %copy-done.4), calls=%async_computation.4 | async-start | bytes 786432 | tf_op jit(solution)/shard_map/all_to_all | solution.py:248
  167.0 1.9 copy-start.2
  168.9 19.7 %copy-start.9 = (bf16[2,64,768]{2,1,0:T(8,128)(2,1)S(1)}, bf16[2,64,768]{2,1,0:T(8,128)(2,1)}, u32[]{:S(2)}) copy-start(bf16[2,64,768]{2,1,0:T(8,128)(2,1)} %get-tuple-element.35.col_out) | copy-start | bytes 589828
Sparse Core Ops, SparseCore 0:
  36.5 43.8 all-gather.4
  82.5 45.1 all-gather.6

commit v6 on v5

--- a/solution.py
+++ b/solution.py
@@ -12,8 +12,9 @@
 ROWS = 128
 COLS = 512
 NEAR = ("ylo", "zlo", "core")
-RED = ("yhi", "zhi")
+RED = ("zhi", "yhi")
 DEP = ("yhi", "ylo", "zhi", "core")
+COLUMN = ("zhi", "yhi", "ylo", "core")
 RES = ("zlo", "x")
 BLOCKS = ("core", "x")
 NHG = 4
@@ -282,7 +283,7 @@
     queries_grads = spread(2)
     mine = mine[:, 2:]
 
-    cols = swap(cols, DEP)
+    cols = swap(cols, COLUMN)
     cols = call(
         column_kernel,
         flat,
@@ -295,7 +296,7 @@
         out_inside="far",
         flops=10**9,
     )
-    cols = swap(cols, DEP)
+    cols = swap(cols, COLUMN)
 
     parts = call(
         logits_kernel,

time: 197 us -> 197 us (level)
  blocking collectives: 58.2 us -> 53.4 us
  starting transfers between devices: 38 us -> 40.3 us
  waiting for transfers between devices: 65.1 us -> 67.2 us
    all_to_all x3, blocking collectives: 58.2 us -> 53.4 us  [swap(): return lax.all_to_all(array, axes, 0, 0, tiled=True)]
    all_to_all x4, starting transfers between devices: 35.2 us -> 37.5 us  [swap(): return lax.all_to_all(array, axes, 0, 0, tiled=True)]
    all_to_all x4, waiting for transfers between devices: 63.2 us -> 65.2 us  [swap(): return lax.all_to_all(array, axes, 0, 0, tiled=True)]
where the time goes in v6:
time: 197 us; the launch traced here: 196 us
  waiting for transfers between devices  67.2 us (34%)
  blocking collectives  53.4 us (27%)
  starting transfers between devices  40.3 us (20%)
  between operations  14.2 us (7%)
  Pallas kernels  13.7 us (7%)
  local copies, waits for them, and re-layouts  5.34 us (3%)
  other arithmetic  2.06 us (1%)
    all_to_all x4, waiting for transfers between devices, swap(): return lax.all_to_all(array, axes, 0, 0, tiled=True)  65.2 us
    all_to_all x3, blocking collectives, swap(): return lax.all_to_all(array, axes, 0, 0, tiled=True)  53.4 us
    all_to_all x4, starting transfers between devices, swap(): return lax.all_to_all(array, axes, 0, 0, tiled=True)  37.5 us
    pallas_call x9, Pallas kernels, call(): pl.pallas_call(body, out_shape=out_shape, in_specs=[spec] * len(args), ou...  13.7 us
    unnamed x20, local copies, waits for them, and re-layouts  5.34 us
  transfers between devices with their start and end apart: 7, of which 5 were waited for; matrix products, arithmetic and copies ran while one was open for 0% of the time, Pallas kernels for 5%

profile of v6, /device:TPU:1, one launch (start us, length us, event | category | flops | bytes accessed | tf_op | source)
XLA Modules:
  0.0 196.1 jit_solution(6951235954371602901)
XLA Ops:
  7.2 2.2 %shard_map.127 = bf16[8,4,3,32,128]{4,3,2,1,0:T(8,128)(2,1)} custom-call(bf16[2,64,768]{2,1,0:T(8,128)(2,1)} %refs_0_.1, bf16[2,64,768]{2,1,0:T(8,128)(2,1)} %refs_1_.1, bf16[2,64,768]{2,1,0:T(8,128)(2,1)} %refs_2_.1, bf16[2,64,768]{2,1,0:T(8,128)(2,1)} %refs_3_.1), custom_call_target="tpu_custom_call" | custom-call | flops 10000000 | bytes 1572864 | tf_op jit(solution)/shard_map/pallas_call | solution.py:48
  9.4 10.3 %all-to-all-start = ((bf16[8,4,3,32,128]{4,3,2,1,0:T(8,128)(2,1)}), bf16[8,4,3,32,128]{4,3,2,1,0:T(8,128)(2,1)S(1)}, u32[]{:S(2)}, u32[]{:S(2)}) async-start(bf16[8,4,3,32,128]{4,3,2,1,0:T(8,128)(2,1)} %shard_map.127), calls=%async_computation | async-start | bytes 1572864 | tf_op jit(solution)/shard_map/all_to_all | solution.py:249
  19.8 1.4 shard_map.126
  21.2 9.4 %all-to-all-done = bf16[8,4,3,32,128]{4,3,2,1,0:T(8,128)(2,1)S(1)} async-done(((bf16[8,4,3,32,128]{4,3,2,1,0:T(8,128)(2,1)}), bf16[8,4,3,32,128]{4,3,2,1,0:T(8,128)(2,1)S(1)}, u32[]{:S(2)}, u32[]{:S(2)}) %all-to-all-start) | async-done | bytes 786464 | tf_op jit(solution)/shard_map/all_to_all | solution.py:249
  30.6 2.8 %collective-permute-start = (bf16[8,4,3,32,128]{4,3,2,1,0:T(8,128)(2,1)S(1)}, bf16[8,4,3,32,128]{4,3,2,1,0:T(8,128)(2,1)S(1)}, u32[]{:S(2)}, u32[]{:S(2)}) collective-permute-start(bf16[8,4,3,32,128]{4,3,2,1,0:T(8,128)(2,1)S(1)} %all-to-all-done), channel_id=1, source_target_pairs={{0,8},{8,0},{1,9},{9,1},{2,10},{10,2},{3,11},{11,3},{4,12},{12,4},... | collective-permute-start | bytes 2359304 | tf_op jit(solution)/shard_map/ppermute | solution.py:275
  33.4 1.9 collective-permute-done
  35.2 0.1 select_bitcast_fusion.1
  35.4 1.0 pad_maximum_fusion
  36.4 11.1 %all-to-all-start.1 = ((bf16[64,8,768]{2,1,0:T(8,128)(2,1)}), bf16[64,8,768]{2,1,0:T(8,128)(2,1)S(1)}, u32[]{:S(2)}, u32[]{:S(2)}) async-start(bf16[64,8,768]{2,1,0:T(8,128)(2,1)} %bitcast), calls=%async_computation.1 | async-start | bytes 1572864 | tf_op jit(solution)/shard_map/all_to_all | solution.py:249
  47.5 0.0 all-gather.7.cloned.1.call-start
  47.6 1.0 pad_maximum_fusion.1
  48.5 0.0 all-gather.7.cloned.1.call-update
  48.6 23.1 %all-to-all-done.1 = bf16[64,8,768]{2,1,0:T(8,128)(2,1)S(1)} async-done(((bf16[64,8,768]{2,1,0:T(8,128)(2,1)}), bf16[64,8,768]{2,1,0:T(8,128)(2,1)S(1)}, u32[]{:S(2)}, u32[]{:S(2)}) %all-to-all-start.1) | async-done | bytes 786464 | tf_op jit(solution)/shard_map/all_to_all | solution.py:249
  71.7 3.9 %shard_map.128 = bf16[512,768]{1,0:T(8,128)(2,1)} custom-call(bf16[512,768]{1,0:T(8,128)(2,1)S(1)} %bitcast.17), custom_call_target="tpu_custom_call" | custom-call | flops 1000000000 | bytes 1572864 | tf_op jit(solution)/shard_map/pallas_call | solution.py:48
  75.5 8.3 %all-to-all-start.2 = ((bf16[64,8,768]{2,1,0:T(8,128)(2,1)}), bf16[64,8,768]{2,1,0:T(8,128)(2,1)}, u32[]{:S(2)}, u32[]{:S(2)}) async-start(bf16[64,8,768]{2,1,0:T(8,128)(2,1)} %bitcast.2), calls=%async_computation.2 | async-start | bytes 1572864 | tf_op jit(solution)/shard_map/all_to_all | solution.py:249
  83.8 0.0 all-gather.5.cloned.1.call-done
  83.9 1.9 copy-done
  85.7 1.1 shard_map.129
  86.9 0.8 copy-done.3
  87.7 20.1 %all-to-all-done.2 = bf16[64,8,768]{2,1,0:T(8,128)(2,1)} async-done(((bf16[64,8,768]{2,1,0:T(8,128)(2,1)}), bf16[64,8,768]{2,1,0:T(8,128)(2,1)}, u32[]{:S(2)}, u32[]{:S(2)}) %all-to-all-start.2) | async-done | bytes 786464 | tf_op jit(solution)/shard_map/all_to_all | solution.py:249
  107.8 23.9 %all_to_all.48.parts = bf16[16,72,256]{2,1,0:T(8,128)(2,1)S(1)} all-to-all(bf16[16,72,256]{2,1,0:T(8,128)(2,1)} %copy-done.3), channel_id=1, replica_groups=mesh['yhi'=4,'ylo'=2,'zhi'=4,'core'=2,'zlo'=2,'x'=4] {'zhi','yhi'}, dimensions={0} | all-to-all | bytes 1179648 | tf_op jit(solution)/shard_map/all_to_all | solution.py:249
  131.8 0.3 shard_map.130
  132.1 0.7 copy-done.4
  132.8 7.7 %all-to-all-start.4 = ((bf16[16,24,512]{2,1,0:T(8,128)(2,1)}), bf16[16,24,512]{2,1,0:T(8,128)(2,1)S(1)}, u32[]{:S(2)}, u32[]{:S(2)}) async-start(bf16[16,24,512]{2,1,0:T(8,128)(2,1)} %copy-done.4), calls=%async_computation.4 | async-start | bytes 786432 | tf_op jit(solution)/shard_map/all_to_all | solution.py:249
  140.5 2.3 %shard_map.131 = (bf16[2,64,768]{2,1,0:T(8,128)(2,1)}, bf16[2,64,768]{2,1,0:T(8,128)(2,1)}, bf16[2,64,768]{2,1,0:T(8,128)(2,1)}, bf16[2,64,768]{2,1,0:T(8,128)(2,1)}) custom-call(bf16[512,768]{1,0:T(8,128)(2,1)} %bitcast.3.columns), custom_call_target="tpu_custom_call" | custom-call | flops 10000000 | bytes 1572864 | tf_op jit(solution)/shard_map/pallas_call | solution.py:48
  142.9 12.6 %all-to-all-done.4.rows = bf16[16,24,512]{2,1,0:T(8,128)(2,1)S(1)} async-done(((bf16[16,24,512]{2,1,0:T(8,128)(2,1)}), bf16[16,24,512]{2,1,0:T(8,128)(2,1)S(1)}, u32[]{:S(2)}, u32[]{:S(2)}) %all-to-all-start.4) | async-done | bytes 393248 | tf_op jit(solution)/shard_map/all_to_all | solution.py:249
  155.5 0.2 shard_map.132
  155.7 14.4 %all_to_all.49.by_query = bf16[8,192,128]{2,1,0:T(8,128)(2,1)S(1)} all-to-all(bf16[8,192,128]{2,1,0:T(8,128)(2,1)S(1)} %get-tuple-element.33), channel_id=1, replica_groups=mesh['yhi'=4,'ylo'=2,'zhi'=4,'core'=2,'zlo'=2,'x'=4] {'core','x'}, dimensions={0} | all-to-all | bytes 786432 | tf_op jit(solution)/shard_map/all_to_all | solution.py:249
  170.1 1.9 copy-done.2
  172.0 1.1 shard_map.133
  173.1 15.0 %all_to_all.50.heads = bf16[8,4,3,32,128]{4,3,2,1,0:T(8,128)(2,1)S(1)} all-to-all(bf16[8,4,3,32,128]{4,3,2,1,0:T(8,128)(2,1)S(1)} %shard_map.133), channel_id=1, replica_groups=mesh['yhi'=4,'ylo'=2,'zhi'=4,'core'=2,'zlo'=2,'x'=4] {'ylo','zlo','core'}, dimensions={0} | all-to-all | bytes 1572864 | tf_op jit(solution)/shard_map/all_to_all | solution.py:249
  188.1 1.1 shard_map.134
  (19 shorter events, 0.1 us)
Async XLA Ops:
  7.2 12.6 %copy-start.5 = (bf16[2,64,768]{2,1,0:T(8,128)(2,1)S(1)}, bf16[2,64,768]{2,1,0:T(8,128)(2,1)}, u32[]{:S(2)}) copy-start(bf16[2,64,768]{2,1,0:T(8,128)(2,1)} %refs_3_.1) | copy-start | bytes 589828
  7.2 12.6 %copy-start.8 = (bf16[2,64,768]{2,1,0:T(8,128)(2,1)S(1)}, bf16[2,64,768]{2,1,0:T(8,128)(2,1)}, u32[]{:S(2)}) copy-start(bf16[2,64,768]{2,1,0:T(8,128)(2,1)} %values.1) | copy-start | bytes 589828
  7.2 12.6 %copy-start.7 = (bf16[2,64,768]{2,1,0:T(8,128)(2,1)S(1)}, bf16[2,64,768]{2,1,0:T(8,128)(2,1)}, u32[]{:S(2)}) copy-start(bf16[2,64,768]{2,1,0:T(8,128)(2,1)} %keys.1) | copy-start | bytes 589828
  7.2 12.6 %copy-start.6 = (bf16[2,64,768]{2,1,0:T(8,128)(2,1)S(1)}, bf16[2,64,768]{2,1,0:T(8,128)(2,1)}, u32[]{:S(2)}) copy-start(bf16[2,64,768]{2,1,0:T(8,128)(2,1)} %query.1) | copy-start | bytes 589828
  9.4 21.1 %all-to-all-start = ((bf16[8,4,3,32,128]{4,3,2,1,0:T(8,128)(2,1)}), bf16[8,4,3,32,128]{4,3,2,1,0:T(8,128)(2,1)S(1)}, u32[]{:S(2)}, u32[]{:S(2)}) async-start(bf16[8,4,3,32,128]{4,3,2,1,0:T(8,128)(2,1)} %shard_map.127), calls=%async_computation | async-start | bytes 1572864 | tf_op jit(solution)/shard_map/all_to_all | solution.py:249
  19.8 64.1 %all-gather.5.cloned.1.call-start = ((), (), s32[]{:S(2)}) async-start(), calls=%async_computation.7 | async-start | bytes 3932160 | tf_op jit(solution)/shard_map/all_gather | solution.py:280
  30.6 4.7 %collective-permute-start = (bf16[8,4,3,32,128]{4,3,2,1,0:T(8,128)(2,1)S(1)}, bf16[8,4,3,32,128]{4,3,2,1,0:T(8,128)(2,1)S(1)}, u32[]{:S(2)}, u32[]{:S(2)}) collective-permute-start(bf16[8,4,3,32,128]{4,3,2,1,0:T(8,128)(2,1)S(1)} %all-to-all-done), channel_id=1, source_target_pairs={{0,8},{8,0},{1,9},{9,1},{2,10},{10,2},{3,11},{11,3},{4,12},{12,4},... | collective-permute-start | bytes 2359304 | tf_op jit(solution)/shard_map/ppermute | solution.py:275
  36.4 35.3 %all-to-all-start.1 = ((bf16[64,8,768]{2,1,0:T(8,128)(2,1)}), bf16[64,8,768]{2,1,0:T(8,128)(2,1)S(1)}, u32[]{:S(2)}, u32[]{:S(2)}) async-start(bf16[64,8,768]{2,1,0:T(8,128)(2,1)} %bitcast), calls=%async_computation.1 | async-start | bytes 1572864 | tf_op jit(solution)/shard_map/all_to_all | solution.py:249
  47.5 95.3 %all-gather.7.cloned.1.call-start = ((), (), s32[]{:S(2)}) async-start(), calls=%async_computation.8 | async-start | bytes 3932160 | tf_op jit(solution)/shard_map/all_gather | solution.py:280
  75.5 32.3 %all-to-all-start.2 = ((bf16[64,8,768]{2,1,0:T(8,128)(2,1)}), bf16[64,8,768]{2,1,0:T(8,128)(2,1)}, u32[]{:S(2)}, u32[]{:S(2)}) async-start(bf16[64,8,768]{2,1,0:T(8,128)(2,1)} %bitcast.2), calls=%async_computation.2 | async-start | bytes 1572864 | tf_op jit(solution)/shard_map/all_to_all | solution.py:249
  83.8 1.9 copy-start
  86.9 0.8 copy-start.3
  87.7 82.4 %copy-start.1 = (bf16[8,8,2,3,32,128]{5,4,3,2,1,0:T(8,128)(2,1)S(1)}, bf16[8,8,2,3,32,128]{5,4,3,2,1,0:T(8,128)(2,1)}, u32[]{:S(2)}) copy-start(bf16[8,8,2,3,32,128]{5,4,3,2,1,0:T(8,128)(2,1)} %all-gather.5.cloned.1.call-done) | copy-start | bytes 9437188
  132.1 0.7 copy-start.4
  132.8 22.6 %all-to-all-start.4 = ((bf16[16,24,512]{2,1,0:T(8,128)(2,1)}), bf16[16,24,512]{2,1,0:T(8,128)(2,1)S(1)}, u32[]{:S(2)}, u32[]{:S(2)}) async-start(bf16[16,24,512]{2,1,0:T(8,128)(2,1)} %copy-done.4), calls=%async_computation.4 | async-start | bytes 786432 | tf_op jit(solution)/shard_map/all_to_all | solution.py:249
  170.1 1.9 copy-start.2
  172.0 16.1 %copy-start.9 = (bf16[2,64,768]{2,1,0:T(8,128)(2,1)S(1)}, bf16[2,64,768]{2,1,0:T(8,128)(2,1)}, u32[]{:S(2)}) copy-start(bf16[2,64,768]{2,1,0:T(8,128)(2,1)} %get-tuple-element.35.col_out) | copy-start | bytes 589828
Sparse Core Ops, SparseCore 0:
  36.5 43.8 all-gather.4
  82.5 45.1 all-gather.6

commit v7 on v6

--- a/solution.py
+++ b/solution.py
@@ -96,17 +96,19 @@
     )
 
 
-def gathered(ref, n, h):
-    return jnp.concatenate(
-        [block(ref, (x, c), n, h) for c in range(NC) for x in range(NX)], axis=0
-    )
-
-
-def logits_kernel(mine, keys_values, out):
+def gathered(refs, n, h):
+    return jnp.concatenate([block(ref, (x,), n, h) for ref in refs for x in range(NX)], axis=0)
+
+
+def place(slot):
+    return (slot // NX + lax.axis_index("core")) % NC * NX + slot % NX
+
+
+def logits_kernel(mine, near, far, out):
     logits, dprobs = [], []
     for h in range(HL):
         for res, n, which in ((logits, 0, 0), (dprobs, 1, 1)):
-            res.append(dot(block(mine, (), n, h), gathered(keys_values, which, h), 1, 1))
+            res.append(dot(block(mine, (), n, h), gathered((near, far), which, h), 1, 1))
     logits = jnp.concatenate(logits, axis=0)
     dprobs = jnp.concatenate(dprobs, axis=0)
     dprobs = dprobs - jnp.mean(dprobs, axis=-1, keepdims=True)
@@ -143,12 +145,12 @@
     probs[...] = p
     dlogits[...] = d
     for r in range(NRES):
-        by_key[r] = jnp.concatenate(
+        by_key[place(r)] = jnp.concatenate(
             [p[:, r * CB : (r + 1) * CB], d[:, r * CB : (r + 1) * CB]], axis=1
         )
 
 
-def row_grads_kernel(probs, dlogits, by_query, keys_values, queries_grads, out):
+def row_grads_kernel(probs, dlogits, by_query, near_kv, far_kv, near_qg, far_qg, out):
 
     def put(n, h, res):
         for z in range(NZ):
@@ -159,11 +161,11 @@
 
     for h in range(HL):
         at = slice(h * CB, (h + 1) * CB)
-        put(0, h, dot(probs[at, :], gathered(keys_values, 1, h), 1, 0))
-        put(1, h, dot(dlogits[at, :], gathered(keys_values, 0, h), 1, 0))
-        lhs = jnp.concatenate([by_query[r, at, :] for r in range(NRES)], axis=0)
-        put(2, h, dot(lhs, gathered(queries_grads, 0, h), 0, 0)[CB:])
-        put(3, h, dot(lhs, gathered(queries_grads, 1, h), 0, 0)[:CB])
+        put(0, h, dot(probs[at, :], gathered((near_kv, far_kv), 1, h), 1, 0))
+        put(1, h, dot(dlogits[at, :], gathered((near_kv, far_kv), 0, h), 1, 0))
+        lhs = jnp.concatenate([by_query[place(r), at, :] for r in range(NRES)], axis=0)
+        put(2, h, dot(lhs, gathered((near_qg, far_qg), 0, h), 0, 0)[CB:])
+        put(3, h, dot(lhs, gathered((near_qg, far_qg), 1, h), 0, 0)[:CB])
 
 
 def by_column_kernel(query, keys, values, grads, out, rows):
@@ -271,19 +273,12 @@
     mine = swap(by_head, NEAR)
     cols = call(by_column_kernel, flat, col_q, col_k, col_v, cotangent, scratch=[room])
     cols, mine = lax.optimization_barrier((cols, mine))
-    first = lax.axis_index("core") == 0
+    near_kv = lax.all_gather(mine[:, :2], "x", axis=0)
     other = lax.ppermute(mine, "core", [(0, 1), (1, 0)])
 
-    def spread(n):
-        own, far = mine[:, n : n + 2], other[:, n : n + 2]
-        both = jnp.stack([jnp.where(first, own, far), jnp.where(first, far, own)])
-        return lax.all_gather(both, "x", axis=0)
-
-    keys_values = spread(0)
-    queries_grads = spread(2)
-    mine = mine[:, 2:]
-
     cols = swap(cols, COLUMN)
+    cols, other, mine = lax.optimization_barrier((cols, other, mine))
+    far_kv = lax.all_gather(other[:, :2], "x", axis=0)
     cols = call(
         column_kernel,
         flat,
@@ -296,13 +291,17 @@
         out_inside="far",
         flops=10**9,
     )
+    cols, other, mine = lax.optimization_barrier((cols, other[:, 2:], mine[:, 2:]))
+    near_qg = lax.all_gather(mine, "x", axis=0)
+    far_qg = lax.all_gather(other, "x", axis=0)
     cols = swap(cols, COLUMN)
 
     parts = call(
         logits_kernel,
         sds((NRED, 6 * QR, COLS // 2), bf),
         mine,
-        keys_values,
+        near_kv,
+        far_kv,
     )
     cols, parts = lax.optimization_barrier((cols, parts))
     parts = swap(parts, RED)
@@ -311,7 +310,9 @@
     col_out, grad_cq, grad_ck, grad_cv = call(
         column_finish_kernel, [dev] * 4, cols, scratch=[room], inside=False
     )
-    rows, queries_grads, col_out = lax.optimization_barrier((rows, queries_grads, col_out))
+    rows, near_qg, far_qg, col_out = lax.optimization_barrier(
+        (rows, near_qg, far_qg, col_out)
+    )
     probs, dlogits, by_key = call(
         assemble_kernel,
         [
@@ -328,8 +329,10 @@
         probs,
         dlogits,
         by_query,
-        keys_values,
-        queries_grads,
+        near_kv,
+        far_kv,
+        near_qg,
+        far_qg,
     )
     back = swap(back, NEAR)
     update, grad_rq, grad_rk, grad_rv = call(

time: 197 us -> 204 us (1.036)
  local copies, waits for them, and re-layouts: 5.34 us -> 9.95 us
  waiting for transfers between devices: 67.2 us -> 71.8 us
  blocking collectives: 53.4 us -> 55.6 us
  other arithmetic: 2.06 us -> 0 us
    all_gather x2 -> x4, waiting for transfers between devices: 0.02 us -> 35.7 us  [the longest x1 20.5 us: on_device(): near_qg = lax.all_gather(mine, 'x', axis=0)]
    all_to_all x4, waiting for transfers between devices: 65.2 us -> 33.6 us  [swap(): return lax.all_to_all(array, axes, 0, 0, tiled=True)]
    slice x0 -> x3, local copies, waits for them, and re-layouts: none -> 2.62 us  [the longest x1 0.96 us: on_device(): far_kv = lax.all_gather(other[:, :2], 'x', axis=0)]
    all_to_all x3, blocking collectives: 53.4 us -> 55.6 us  [swap(): return lax.all_to_all(array, axes, 0, 0, tiled=True)]
    another operation x3 -> x0, other arithmetic: 2.06 us -> none  [spread(): both = jnp.stack([jnp.where(first, own, far), jnp.where(first, far, own)])]
    unnamed x20 -> x28, local copies, waits for them, and re-layouts: 5.34 us -> 7.33 us
  transfers between devices with their start and end apart: 7 -> 9, of which waited for: 5 -> 6; matrix products, arithmetic and copies ran while one was open for 0% -> 1% of each run, Pallas kernels for 5% -> 4%
where the time goes in v7:
time: 204 us
  waiting for transfers between devices  71.8 us (35%)
  blocking collectives  55.6 us (27%)
  starting transfers between devices  38.8 us (19%)
  between operations  13.9 us (7%)
  Pallas kernels  13.7 us (7%)
  local copies, waits for them, and re-layouts  9.95 us (5%)
    all_to_all x3, blocking collectives, swap(): return lax.all_to_all(array, axes, 0, 0, tiled=True)  55.6 us
    all_to_all x4, starting transfers between devices, swap(): return lax.all_to_all(array, axes, 0, 0, tiled=True)  36.3 us
    all_to_all x4, waiting for transfers between devices, swap(): return lax.all_to_all(array, axes, 0, 0, tiled=True)  33.6 us
    all_gather x1, waiting for transfers between devices, on_device(): near_qg = lax.all_gather(mine, 'x', axis=0)  20.5 us
    all_gather x1, waiting for transfers between devices, on_device(): far_kv = lax.all_gather(other[:, :2], 'x', axis=0)  15.2 us
    pallas_call x9, Pallas kernels, call(): pl.pallas_call(body, out_shape=out_shape, in_specs=[spec] * len(args), ou...  13.7 us
    unnamed x28, local copies, waits for them, and re-layouts  7.33 us
  transfers between devices with their start and end apart: 9, of which 6 were waited for; matrix products, arithmetic and copies ran while one was open for 1% of the time, Pallas kernels for 4%

profile of v7, /device:TPU:1, one launch (start us, length us, event | category | flops | bytes accessed | tf_op | source)
XLA Modules:
  0.0 203.7 jit_solution(4442385219169153827)
XLA Ops:
  7.2 2.3 %shard_map.127 = bf16[8,4,3,32,128]{4,3,2,1,0:T(8,128)(2,1)} custom-call(bf16[2,64,768]{2,1,0:T(8,128)(2,1)} %refs_0_.1, bf16[2,64,768]{2,1,0:T(8,128)(2,1)} %refs_1_.1, bf16[2,64,768]{2,1,0:T(8,128)(2,1)} %refs_2_.1, bf16[2,64,768]{2,1,0:T(8,128)(2,1)} %refs_3_.1), custom_call_target="tpu_custom_call" | custom-call | flops 10000000 | bytes 1572864 | tf_op jit(solution)/shard_map/pallas_call | solution.py:48
  9.5 10.3 %all-to-all-start = ((bf16[8,4,3,32,128]{4,3,2,1,0:T(8,128)(2,1)}), bf16[8,4,3,32,128]{4,3,2,1,0:T(8,128)(2,1)S(1)}, u32[]{:S(2)}, u32[]{:S(2)}) async-start(bf16[8,4,3,32,128]{4,3,2,1,0:T(8,128)(2,1)} %shard_map.127), calls=%async_computation | async-start | bytes 1572864 | tf_op jit(solution)/shard_map/all_to_all | solution.py:251
  19.8 1.3 shard_map.126
  21.2 9.4 %all-to-all-done = bf16[8,4,3,32,128]{4,3,2,1,0:T(8,128)(2,1)S(1)} async-done(((bf16[8,4,3,32,128]{4,3,2,1,0:T(8,128)(2,1)}), bf16[8,4,3,32,128]{4,3,2,1,0:T(8,128)(2,1)S(1)}, u32[]{:S(2)}, u32[]{:S(2)}) %all-to-all-start) | async-done | bytes 786464 | tf_op jit(solution)/shard_map/all_to_all | solution.py:251
  30.6 0.8 slice.14
  31.5 11.6 %all-to-all-start.1 = ((bf16[64,8,768]{2,1,0:T(8,128)(2,1)}), bf16[64,8,768]{2,1,0:T(8,128)(2,1)S(1)}, u32[]{:S(2)}, u32[]{:S(2)}) async-start(bf16[64,8,768]{2,1,0:T(8,128)(2,1)} %bitcast), calls=%async_computation.1 | async-start | bytes 1572864 | tf_op jit(solution)/shard_map/all_to_all | solution.py:251
  43.2 2.4 %collective-permute-start = (bf16[8,4,3,32,128]{4,3,2,1,0:T(8,128)(2,1)S(1)}, bf16[8,4,3,32,128]{4,3,2,1,0:T(8,128)(2,1)S(1)}, u32[]{:S(2)}, u32[]{:S(2)}) collective-permute-start(bf16[8,4,3,32,128]{4,3,2,1,0:T(8,128)(2,1)S(1)} %all-to-all-done), channel_id=1, source_target_pairs={{0,8},{8,0},{1,9},{9,1},{2,10},{10,2},{3,11},{11,3},{4,12},{12,4},... | collective-permute-start | bytes 2359304 | tf_op jit(solution)/shard_map/ppermute | solution.py:277
  45.5 1.9 collective-permute-done
  47.4 19.8 %all-to-all-done.1 = bf16[64,8,768]{2,1,0:T(8,128)(2,1)S(1)} async-done(((bf16[64,8,768]{2,1,0:T(8,128)(2,1)}), bf16[64,8,768]{2,1,0:T(8,128)(2,1)S(1)}, u32[]{:S(2)}, u32[]{:S(2)}) %all-to-all-start.1) | async-done | bytes 786464 | tf_op jit(solution)/shard_map/all_to_all | solution.py:251
  67.3 1.0 fusion
  68.3 0.8 slice.13.mine
  69.1 3.9 %shard_map.128 = bf16[512,768]{1,0:T(8,128)(2,1)} custom-call(bf16[512,768]{1,0:T(8,128)(2,1)S(1)} %bitcast.14), custom_call_target="tpu_custom_call" | custom-call | flops 1000000000 | bytes 1572864 | tf_op jit(solution)/shard_map/pallas_call | solution.py:48
  73.0 8.2 %all-to-all-start.2 = ((bf16[64,8,768]{2,1,0:T(8,128)(2,1)}), bf16[64,8,768]{2,1,0:T(8,128)(2,1)S(1)}, u32[]{:S(2)}, u32[]{:S(2)}) async-start(bf16[64,8,768]{2,1,0:T(8,128)(2,1)} %bitcast.2), calls=%async_computation.2 | async-start | bytes 1572864 | tf_op jit(solution)/shard_map/all_to_all | solution.py:251
  81.3 0.5 all-gather.13.cloned.1.call-update
  81.9 15.2 %all-gather.11.cloned.1.call-done = bf16[32,2,3,32,128]{4,3,2,1,0:T(8,128)(2,1)} async-done(((bf16[8,2,3,32,128]{4,3,2,1,0:T(8,128)(2,1)}), bf16[32,2,3,32,128]{4,3,2,1,0:T(8,128)(2,1)}) %all-gather.11.cloned.1.call-update) | async-done | bytes 1572880 | tf_op jit(solution)/shard_map/all_gather | solution.py:281
  97.1 1.4 copy-done
  98.5 1.4 copy-done.2
  99.9 1.2 shard_map.129
  101.0 4.3 %all-to-all-done.2 = bf16[64,8,768]{2,1,0:T(8,128)(2,1)S(1)} async-done(((bf16[64,8,768]{2,1,0:T(8,128)(2,1)}), bf16[64,8,768]{2,1,0:T(8,128)(2,1)S(1)}, u32[]{:S(2)}, u32[]{:S(2)}) %all-to-all-start.2) | async-done | bytes 786464 | tf_op jit(solution)/shard_map/all_to_all | solution.py:251
  105.4 0.9 copy-done.13
  106.2 28.9 %all_to_all.49.parts = bf16[16,72,256]{2,1,0:T(8,128)(2,1)S(1)} all-to-all(bf16[16,72,256]{2,1,0:T(8,128)(2,1)S(1)} %shard_map.129), channel_id=1, replica_groups=mesh['yhi'=4,'ylo'=2,'zhi'=4,'core'=2,'zlo'=2,'x'=4] {'zhi','yhi'}, dimensions={0} | all-to-all | bytes 1179648 | tf_op jit(solution)/shard_map/all_to_all | solution.py:251
  135.1 0.3 shard_map.130
  135.5 0.8 copy-done.5
  136.3 6.0 %all-to-all-start.4 = ((bf16[16,24,512]{2,1,0:T(8,128)(2,1)}), bf16[16,24,512]{2,1,0:T(8,128)(2,1)S(1)}, u32[]{:S(2)}, u32[]{:S(2)}) async-start(bf16[16,24,512]{2,1,0:T(8,128)(2,1)} %copy-done.5), calls=%async_computation.4 | async-start | bytes 786432 | tf_op jit(solution)/shard_map/all_to_all | solution.py:251
  142.3 2.3 %shard_map.131 = (bf16[2,64,768]{2,1,0:T(8,128)(2,1)}, bf16[2,64,768]{2,1,0:T(8,128)(2,1)}, bf16[2,64,768]{2,1,0:T(8,128)(2,1)}, bf16[2,64,768]{2,1,0:T(8,128)(2,1)}) custom-call(bf16[512,768]{1,0:T(8,128)(2,1)} %bitcast.15), custom_call_target="tpu_custom_call" | custom-call | flops 10000000 | bytes 1572864 | tf_op jit(solution)/shard_map/pallas_call | solution.py:48
  144.6 20.5 %all-gather.13.cloned.1.call-done = bf16[32,2,3,32,128]{4,3,2,1,0:T(8,128)(2,1)} async-done(((bf16[8,2,3,32,128]{4,3,2,1,0:T(8,128)(2,1)}), bf16[32,2,3,32,128]{4,3,2,1,0:T(8,128)(2,1)}) %all-gather.13.cloned.1.call-update) | async-done | bytes 1572880 | tf_op jit(solution)/shard_map/all_gather | solution.py:295
  165.4 11.5 %all_to_all.50.by_query = bf16[8,192,128]{2,1,0:T(8,128)(2,1)S(1)} all-to-all(bf16[8,192,128]{2,1,0:T(8,128)(2,1)S(1)} %get-tuple-element.46), channel_id=1, replica_groups=mesh['yhi'=4,'ylo'=2,'zhi'=4,'core'=2,'zlo'=2,'x'=4] {'core','x'}, dimensions={0} | all-to-all | bytes 786432 | tf_op jit(solution)/shard_map/all_to_all | solution.py:251
  176.9 1.4 copy-done.6
  178.3 1.4 copy-done.7
  179.7 1.1 shard_map.133
  180.9 15.2 %all_to_all.51.heads = bf16[8,4,3,32,128]{4,3,2,1,0:T(8,128)(2,1)S(1)} all-to-all(bf16[8,4,3,32,128]{4,3,2,1,0:T(8,128)(2,1)S(1)} %shard_map.133), channel_id=1, replica_groups=mesh['yhi'=4,'ylo'=2,'zhi'=4,'core'=2,'zlo'=2,'x'=4] {'ylo','zlo','core'}, dimensions={0} | all-to-all | bytes 1572864 | tf_op jit(solution)/shard_map/all_to_all | solution.py:251
  196.0 1.1 shard_map.134
  (33 shorter events, 0.4 us)
Async XLA Ops:
  7.2 12.6 %copy-start.8 = (bf16[2,64,768]{2,1,0:T(8,128)(2,1)S(1)}, bf16[2,64,768]{2,1,0:T(8,128)(2,1)}, u32[]{:S(2)}) copy-start(bf16[2,64,768]{2,1,0:T(8,128)(2,1)} %refs_3_.1) | copy-start | bytes 589828
  7.2 12.6 %copy-start.11 = (bf16[2,64,768]{2,1,0:T(8,128)(2,1)S(1)}, bf16[2,64,768]{2,1,0:T(8,128)(2,1)}, u32[]{:S(2)}) copy-start(bf16[2,64,768]{2,1,0:T(8,128)(2,1)} %values.1) | copy-start | bytes 589828
  7.2 12.6 %copy-start.10 = (bf16[2,64,768]{2,1,0:T(8,128)(2,1)S(1)}, bf16[2,64,768]{2,1,0:T(8,128)(2,1)}, u32[]{:S(2)}) copy-start(bf16[2,64,768]{2,1,0:T(8,128)(2,1)} %keys.1) | copy-start | bytes 589828
  7.2 12.6 %copy-start.9 = (bf16[2,64,768]{2,1,0:T(8,128)(2,1)S(1)}, bf16[2,64,768]{2,1,0:T(8,128)(2,1)}, u32[]{:S(2)}) copy-start(bf16[2,64,768]{2,1,0:T(8,128)(2,1)} %query.1) | copy-start | bytes 589828
  9.5 21.1 %all-to-all-start = ((bf16[8,4,3,32,128]{4,3,2,1,0:T(8,128)(2,1)}), bf16[8,4,3,32,128]{4,3,2,1,0:T(8,128)(2,1)S(1)}, u32[]{:S(2)}, u32[]{:S(2)}) async-start(bf16[8,4,3,32,128]{4,3,2,1,0:T(8,128)(2,1)} %shard_map.127), calls=%async_computation | async-start | bytes 1572864 | tf_op jit(solution)/shard_map/all_to_all | solution.py:251
  19.8 62.1 %all-gather.9.cloned.1.call-start = ((), (), s32[]{:S(2)}) async-start(), calls=%async_computation.7 | async-start | bytes 1966080 | tf_op jit(solution)/shard_map/all_gather | solution.py:276
  31.5 35.8 %all-to-all-start.1 = ((bf16[64,8,768]{2,1,0:T(8,128)(2,1)}), bf16[64,8,768]{2,1,0:T(8,128)(2,1)S(1)}, u32[]{:S(2)}, u32[]{:S(2)}) async-start(bf16[64,8,768]{2,1,0:T(8,128)(2,1)} %bitcast), calls=%async_computation.1 | async-start | bytes 1572864 | tf_op jit(solution)/shard_map/all_to_all | solution.py:251
  43.1 53.9 %all-gather.11.cloned.1.call-start = ((), (), s32[]{:S(2)}) async-start(), calls=%async_computation.8 | async-start | bytes 1966080 | tf_op jit(solution)/shard_map/all_gather | solution.py:281
  43.2 4.3 %collective-permute-start = (bf16[8,4,3,32,128]{4,3,2,1,0:T(8,128)(2,1)S(1)}, bf16[8,4,3,32,128]{4,3,2,1,0:T(8,128)(2,1)S(1)}, u32[]{:S(2)}, u32[]{:S(2)}) collective-permute-start(bf16[8,4,3,32,128]{4,3,2,1,0:T(8,128)(2,1)S(1)} %all-to-all-done), channel_id=1, source_target_pairs={{0,8},{8,0},{1,9},{9,1},{2,10},{10,2},{3,11},{11,3},{4,12},{12,4},... | collective-permute-start | bytes 2359304 | tf_op jit(solution)/shard_map/ppermute | solution.py:277
  68.2 76.4 %all-gather.15.cloned.1.call-start = ((), (), s32[]{:S(2)}) async-start(), calls=%async_computation.10 | async-start | bytes 1966080 | tf_op jit(solution)/shard_map/all_gather | solution.py:296
  73.0 24.1 %copy-start.4 = (bf16[8,2,3,32,128]{4,3,2,1,0:T(8,128)(2,1)S(1)}, bf16[8,2,3,32,128]{4,3,2,1,0:T(8,128)(2,1)}, u32[]{:S(2)}) copy-start(bf16[8,2,3,32,128]{4,3,2,1,0:T(8,128)(2,1)} %slice.13.mine) | copy-start | bytes 1179652
  73.0 32.3 %all-to-all-start.2 = ((bf16[64,8,768]{2,1,0:T(8,128)(2,1)}), bf16[64,8,768]{2,1,0:T(8,128)(2,1)S(1)}, u32[]{:S(2)}, u32[]{:S(2)}) async-start(bf16[64,8,768]{2,1,0:T(8,128)(2,1)} %bitcast.2), calls=%async_computation.2 | async-start | bytes 1572864 | tf_op jit(solution)/shard_map/all_to_all | solution.py:251
  81.3 83.9 %all-gather.13.cloned.1.call-start = ((), (), s32[]{:S(2)}) async-start(), calls=%async_computation.9 | async-start | bytes 1966080 | tf_op jit(solution)/shard_map/all_gather | solution.py:295
  97.1 1.4 copy-start
  98.5 1.4 copy-start.2
  105.4 0.9 copy-start.13
  135.1 41.8 %copy-start.3 = (bf16[32,2,3,32,128]{4,3,2,1,0:T(8,128)(2,1)S(1)}, bf16[32,2,3,32,128]{4,3,2,1,0:T(8,128)(2,1)}, u32[]{:S(2)}) copy-start(bf16[32,2,3,32,128]{4,3,2,1,0:T(8,128)(2,1)} %all-gather.11.cloned.1.call-done) | copy-start | bytes 4718596
  135.5 0.8 copy-start.5
  136.3 40.6 %copy-start.1 = (bf16[32,2,3,32,128]{4,3,2,1,0:T(8,128)(2,1)S(1)}, bf16[32,2,3,32,128]{4,3,2,1,0:T(8,128)(2,1)}, u32[]{:S(2)}) copy-start(bf16[32,2,3,32,128]{4,3,2,1,0:T(8,128)(2,1)} %all-gather.9.cloned.1.call-done) | copy-start | bytes 4718596
  136.3 28.9 %all-to-all-start.4 = ((bf16[16,24,512]{2,1,0:T(8,128)(2,1)}), bf16[16,24,512]{2,1,0:T(8,128)(2,1)S(1)}, u32[]{:S(2)}, u32[]{:S(2)}) async-start(bf16[16,24,512]{2,1,0:T(8,128)(2,1)} %copy-done.5), calls=%async_computation.4 | async-start | bytes 786432 | tf_op jit(solution)/shard_map/all_to_all | solution.py:251
  176.9 1.4 copy-start.6
  178.3 1.4 copy-start.7
  180.8 15.2 %copy-start.12 = (bf16[2,64,768]{2,1,0:T(8,128)(2,1)S(1)}, bf16[2,64,768]{2,1,0:T(8,128)(2,1)}, u32[]{:S(2)}) copy-start(bf16[2,64,768]{2,1,0:T(8,128)(2,1)} %get-tuple-element.49.col_out) | copy-start | bytes 589828
Sparse Core Ops, SparseCore 0:
  31.6 31.3 all-gather.8
  68.4 28.6 all-gather.10
  99.2 31.9 all-gather.14
  133.1 32.0 all-gather.12
